TPU v7x, 32 devices: a whole 2x2x4 slice. The times are simulated.
32 devices in a mesh: dp: 8 (over y, x, core), tensor: 4 (over z).
Axes of the slice: x: 2, y: 2, z: 4, core: 2. Of those that a mesh axis runs over, the one named last changes fastest.
Arguments:
- base_codes: int32 [4096, 14336], P('dp', 'tensor'), may hold values from 0 to 15
- block_scales: float32 [4096, 224], P('dp', 'tensor'), may hold values from 0.0008 to 0.0176, as said below
- input_adapter_factor: bfloat16 [4096, 64], replicated, may hold values from -0.09375 to 0.09375
- output_adapter_factor: bfloat16 [64, 14336], P(None, 'tensor'), may hold values from -0.046875 to 0.046875
- magnitude: float32 [14336], P('tensor'), may hold values from 0.5 to 2
- inputs: bfloat16 [1536, 4096], P('dp', 'tensor'), may hold values from -6 to 6
- grad_out: bfloat16 [1536, 14336], P('dp', 'tensor'), may hold values from -1.5 to 1.5
- pre_scale: bfloat16 [1536, 14336], P('dp', 'tensor'), may hold values from -6 to 6
Outputs:
- grad_inputs: bfloat16 [1536, 4096], P('dp', 'tensor')
- input_adapter_gradient: float32 [4096, 64], P('tensor')
- output_adapter_gradient: float32 [64, 14336], P(None, 'tensor')
- grad_magnitude: float32 [14336], P('tensor')
Inputs may be any that keep to these rules, and one draw needn't show every extreme that they name: `block_scales`: block scales of the 4-bit codes.
All inputs are finite; a program needn't handle non-finite values.
Results may differ from a plain program's by a relative error of at most 0.015.
Values may be sent and summed in bfloat16 or wider, within the bound.
A program may use at most 192 MiB of HBM per device.

v0:
```python
import jax
import jax.numpy as jnp
from jax import lax
from jax.sharding import PartitionSpec as P

adapter_scale_factor = 0.5


def on_device(
    base_codes,
    block_scales,
    input_adapter_factor,
    output_adapter_factor,
    magnitude,
    inputs,
    grad_out,
    pre_scale,
):
    row_count = base_codes.shape[0]
    block_size = base_codes.shape[1] // block_scales.shape[1]
    expanded = jnp.repeat(block_scales, block_size, axis=1)
    dequantized_weight = (base_codes.astype(jnp.float32) - 7.5) * expanded
    first_row = lax.axis_index("dp") * row_count
    adapter_row_block = lax.dynamic_slice_in_dim(input_adapter_factor, first_row, row_count, 0)
    merged_weight_matrix = (
        dequantized_weight
        + adapter_scale_factor
        * jnp.dot(adapter_row_block, output_adapter_factor, preferred_element_type=jnp.float32)
    ).astype(jnp.bfloat16)
    grad_f = grad_out.astype(jnp.float32)
    gathered = lax.all_gather(merged_weight_matrix, "dp", axis=0, tiled=True)
    whole_f = gathered.astype(jnp.float32)
    col_norm = jnp.sqrt(jnp.sum(whole_f * whole_f, axis=0) + 1e-06)
    col_norm, scaled_weight_matrix = (
        col_norm,
        (grad_f * (magnitude / col_norm)).astype(jnp.bfloat16),
    )
    partial_value = jnp.einsum(
        "tf,rf->tr", scaled_weight_matrix, gathered, preferred_element_type=jnp.float32
    )
    grad_inputs = lax.psum_scatter(
        partial_value.astype(jnp.bfloat16), "tensor", scatter_dimension=1, tiled=True
    )
    quarter_d = inputs.shape[1]
    offset = lax.axis_index("tensor") * quarter_d
    adapter_part = lax.dynamic_slice_in_dim(input_adapter_factor, offset, quarter_d, 0)
    hidden_lowrank_term = lax.psum(
        jnp.dot(inputs, adapter_part, preferred_element_type=jnp.float32).astype(jnp.bfloat16),
        "tensor",
    )
    back_part = jnp.einsum(
        "tf,rf->tr", scaled_weight_matrix, output_adapter_factor, preferred_element_type=jnp.float32
    )
    backward_lowrank_term = lax.psum(back_part.astype(jnp.bfloat16), "tensor")
    gradient_factor_first = adapter_scale_factor * jnp.einsum(
        "td,tr->dr", inputs, backward_lowrank_term, preferred_element_type=jnp.float32
    )
    gradient_factor_second = adapter_scale_factor * jnp.einsum(
        "tr,tf->rf", hidden_lowrank_term, scaled_weight_matrix, preferred_element_type=jnp.float32
    )
    grad_m = jnp.sum(grad_f * pre_scale.astype(jnp.float32), axis=0) / col_norm
    gradient_factor_first, gradient_factor_second, grad_m = lax.psum(
        (gradient_factor_first, gradient_factor_second, grad_m), "dp"
    )
    return (grad_inputs, gradient_factor_first, gradient_factor_second, grad_m)


def solution(mesh):
    in_specs = (
        P("dp", "tensor"),
        P("dp", "tensor"),
        P(),
        P(None, "tensor"),
        P("tensor"),
        P("dp", "tensor"),
        P("dp", "tensor"),
        P("dp", "tensor"),
    )
    out_specs = (P("dp", "tensor"), P("tensor", None), P(None, "tensor"), P("tensor"))
    return jax.shard_map(
        on_device, mesh=mesh, in_specs=in_specs, out_specs=out_specs, check_vma=False
    )
```

profile of v0, /device:TPU:12, one launch (start us, length us, event | category | flops | bytes accessed | tf_op | source)
XLA Modules:
  0.0 308.3 jit_solution(9064215953050259439)
XLA Ops:
  7.2 0.0 copy-start
  7.2 0.0 all-gather.2.cloned.1.call-start
  7.2 4.9 %broadcast_in_dim.4 = f32[512,56,64]{0,2,1:T(8,128)} broadcast(f32[512,56]{0,1:T(8,128)} %param.9), dimensions={0,1} | broadcast | bytes 7454720 | tf_op jit(solution)/shard_map/broadcast_in_dim | solution.py:21
  12.1 0.0 copy-start.3
  12.1 8.5 %copy.13 = f32[512,3584]{1,0:T(8,128)} copy(f32[512,3584]{0,1:T(8,128)} %bitcast.12) | data formatting | bytes 14680064 | tf_op jit(solution)/shard_map/reshape | solution.py:21
  20.6 0.0 copy-done
  20.6 0.0 copy-done.3
  20.6 8.5 %add_convert_fusion = bf16[512,3584]{1,0:T(8,128)(2,1)} fusion(f32[512,3584]{1,0:T(8,128)} %copy.13, s32[512,3584]{1,0:T(8,128)} %param.8, bf16[64,3584]{1,0:T(8,128)(2,1)S(1)} %copy-done.3, bf16[4096,64]{0,1:T(8,128)(2,1)S(1)} %copy-done, s32[]{:T(128)S(6)} %select_n.6), kind=kOutput, calls=%fused_computation.1 | convolution fusion | flops 245891072 | bytes 18874372 | tf_op jit(solution)/shard_map/dot_general | solution.py:28
  29.1 0.0 copy-start.2
  29.1 0.0 copy-start.1
  29.1 0.0 all-gather.2.cloned.1.call-update
  29.1 0.0 all-reduce.4.cloned.1.call-start
  29.2 0.9 copy-done.2
  30.1 0.2 fusion.3
  30.3 0.2 copy-done.1
  30.6 1.7 fusion.1
  32.3 0.0 copy-start.4
  32.3 140.2 %all-gather.2.cloned.1.call-done = bf16[4096,3584]{1,0:T(8,128)(2,1)} async-done(((bf16[512,3584]{1,0:T(8,128)(2,1)}), bf16[4096,3584]{1,0:T(8,128)(2,1)}) %all-gather.2.cloned.1.call-update) | async-done | bytes 29360144 | tf_op jit(solution)/shard_map/all_gather | solution.py:31
  172.5 10.5 %multiply_reduce_fusion = f32[3584]{0:T(1024)S(1)} fusion(bf16[4096,3584]{1,0:T(8,128)(2,1)} %all-gather.2.cloned.1.call-done), kind=kLoop, calls=%fused_computation | loop fusion | flops 44036608 | bytes 29374464 | tf_op jit(solution)/shard_map/reduce_sum | solution.py:33
  183.0 0.0 copy-done.4
  183.0 0.5 convolution_convert_fusion.1
  183.5 16.4 %all-reduce.1 = (bf16[192,64]{1,0:T(8,128)(2,1)S(1)}, bf16[192,64]{0,1:T(8,128)(2,1)S(1)}) all-reduce(bf16[192,64]{1,0:T(8,128)(2,1)S(1)} %convolution_convert_fusion.1, bf16[192,64]{0,1:T(8,128)(2,1)S(1)} %fusion.3), channel_id=1, replica_groups=mesh['dp'=8,'tensor'=4] {'tensor'}, use_global_device_ids=true, to_apply=%region_2.0 | all-reduce | flops 24576 | bytes 98304 | tf_op jit(solution)/shard_map/psum | solution.py:54
  200.0 1.4 convolution_multiply_fusion
  201.4 0.9 fusion.2
  202.3 0.0 all-reduce.4.cloned.1.call-update
  202.3 0.0 reduce-scatter.2.cloned.1.call-start
  202.4 16.2 %convolution_convert_fusion = bf16[192,4096]{1,0:T(8,128)(2,1)} fusion(bf16[4096,3584]{1,0:T(8,128)(2,1)} %all-gather.2.cloned.1.call-done, bf16[192,3584]{1,0:T(8,128)(2,1)S(1)} %copy-done.1, f32[3584]{0:T(1024)S(1)} %get-tuple-element.9), kind=kOutput, calls=%fused_computation.2 | convolution fusion | flops 5639995392 | bytes 32323584 | tf_op jit(solution)/shard_map/tf,rf->tr/dot_general | solution.py:38
  218.5 0.0 reduce-scatter.2.cloned.1.call-update
  218.6 23.0 %psum.39 = f32[3584]{0:T(1024)} all-reduce(f32[3584]{0:T(1024)S(1)} %get-tuple-element.8), channel_id=1, replica_groups=mesh['dp'=8,'tensor'=4] {'dp'}, use_global_device_ids=true, to_apply=%region_7.0 | all-reduce | flops 3584 | bytes 28672 | tf_op jit(solution)/shard_map/psum | solution.py:62
  241.6 19.0 %all-reduce.4.cloned.1.call-done = (f32[1024,64]{0,1:T(8,128)}, f32[64,3584]{1,0:T(8,128)}) async-done(((f32[1024,64]{0,1:T(8,128)}, f32[64,3584]{1,0:T(8,128)}), (f32[1024,64]{0,1:T(8,128)}, f32[64,3584]{1,0:T(8,128)})) %all-reduce.4.cloned.1.call-update) | async-done | bytes 1179664 | tf_op jit(solution)/shard_map/psum | solution.py:62
  260.6 37.3 %reduce-scatter.2.cloned.1.call-done = bf16[192,1024]{1,0:T(8,128)(2,1)} async-done(((bf16[192,4096]{1,0:T(8,128)(2,1)}), bf16[192,1024]{1,0:T(8,128)(2,1)}) %reduce-scatter.2.cloned.1.call-update) | async-done | bytes 393232 | tf_op jit(solution)/shard_map/reduce_scatter | solution.py:41
  297.9 1.7 copy.16
  299.6 2.2 copy.17
  (1 shorter events, 0.0 us)
Async XLA Ops:
  7.2 13.4 %copy-start = (bf16[4096,64]{0,1:T(8,128)(2,1)S(1)}, bf16[4096,64]{0,1:T(8,128)(2,1)}, u32[]{:S(2)}) copy-start(bf16[4096,64]{0,1:T(8,128)(2,1)} %param.10) | copy-start | bytes 1572868
  7.2 165.4 %all-gather.2.cloned.1.call-start = ((), (), s32[]{:S(2)}) async-start(), calls=%async_computation.1 | async-start | bytes 33030144 | tf_op jit(solution)/shard_map/all_gather | solution.py:31
  12.1 8.5 %copy-start.3 = (bf16[64,3584]{1,0:T(8,128)(2,1)S(1)}, bf16[64,3584]{1,0:T(8,128)(2,1)}, u32[]{:S(2)}) copy-start(bf16[64,3584]{1,0:T(8,128)(2,1)} %param.11) | copy-start | bytes 1376260
  29.1 1.0 copy-start.2
  29.1 1.5 copy-start.1
  29.1 231.5 %all-reduce.4.cloned.1.call-start = ((), (), s32[]{:S(2)}) async-start(), calls=%async_computation.3 | async-start | bytes 2359296 | tf_op jit(solution)/shard_map/psum | solution.py:62
  32.3 150.7 %copy-start.4 = (f32[3584]{0:T(1024)S(1)}, f32[3584]{0:T(1024)}, u32[]{:S(2)}) copy-start(f32[3584]{0:T(1024)} %param.12) | copy-start | bytes 43012
  202.3 95.6 %reduce-scatter.2.cloned.1.call-start = ((), (), s32[]{:S(2)}) async-start(), calls=%async_computation.2 | async-start | bytes 1966080 | tf_op jit(solution)/shard_map/reduce_scatter | solution.py:41
Sparse Core Ops, SparseCore 0:
  29.2 143.2 all-gather.1
  202.4 58.1 all-reduce.3
  263.6 34.2 reduce-scatter.1
where the time goes:
time: 311 us; the launch traced here: 308 us
  waiting for transfers between devices  197 us (63%)
  blocking collectives  39.5 us (13%)
  matrix products  27.7 us (9%)
  local copies, waits for them, and re-layouts  18.4 us (6%)
  between operations  13.8 us (4%)
  other arithmetic  12.2 us (4%)
    all_gather x1, waiting for transfers between devices, on_device(): gathered = lax.all_gather(merged_weight_matrix, 'dp', axis=0, tiled=True)  140 us
    reduce_scatter x1, waiting for transfers between devices, on_device(): lax.psum_scatter(partial_value.astype(jnp.bfloat16), 'tensor', scatter_di...  37.3 us
    psum x1, blocking collectives, on_device(): lax.psum((gradient_factor_first, gradient_factor_second, grad_m), 'dp')  23 us
    psum x1, waiting for transfers between devices, on_device(): lax.psum((gradient_factor_first, gradient_factor_second, grad_m), 'dp')  19 us
    psum x1, blocking collectives, on_device(): backward_lowrank_term = lax.psum(back_part.astype(jnp.bfloat16), 'tensor')  16.4 us
    dot_general x1, matrix products, on_device(): jnp.einsum('tf,rf->tr', scaled_weight_matrix, gathered, preferred_element...  16.2 us
    reduce_sum x1, other arithmetic, on_device(): col_norm = jnp.sqrt(jnp.sum(whole_f * whole_f, axis=0) + 1e-06)  10.5 us
    dot_general x1, matrix products, on_device(): jnp.dot(adapter_row_block, output_adapter_factor, preferred_element_type=...  8.48 us
  transfers between devices with their start and end apart: 3, of which 3 were waited for; matrix products, arithmetic and copies ran while one was open for 6% of the time, Pallas kernels for 0%

commit v1 on v0

v1 whole, which is shorter than its diff:
```python
import jax
import jax.numpy as jnp
from jax import lax
from jax.sharding import PartitionSpec as P

adapter_scale_factor = 0.5


def on_device(
    base_codes,
    block_scales,
    input_adapter_factor,
    output_adapter_factor,
    magnitude,
    inputs,
    grad_out,
    pre_scale,
):
    f32, bf16 = jnp.float32, jnp.bfloat16
    row_count, columns = base_codes.shape
    tokens = grad_out.shape[0]
    dp = lax.axis_index("dp")
    block_size = columns // block_scales.shape[1]
    gathered = lax.all_gather(grad_out, "dp", axis=0, tiled=True)
    quarter_d = inputs.shape[1]
    adapter_part = lax.dynamic_slice_in_dim(
        input_adapter_factor, lax.axis_index("tensor") * quarter_d, quarter_d, 0
    )
    hidden_low = lax.psum(
        jnp.dot(inputs, adapter_part, preferred_element_type=f32).astype(bf16), "tensor"
    )
    hidden_all = lax.all_gather(hidden_low, "dp", axis=0, tiled=True)
    expanded = jnp.repeat(block_scales, block_size, axis=1)
    adapter_row_block = lax.dynamic_slice_in_dim(
        input_adapter_factor, dp * row_count, row_count, 0
    )
    merged = (
        (base_codes.astype(f32) - 7.5) * expanded
        + adapter_scale_factor
        * jnp.dot(adapter_row_block, output_adapter_factor, preferred_element_type=f32)
    ).astype(bf16)
    merged_f = merged.astype(f32)
    column_sums = jnp.sum(merged_f * merged_f, axis=0)
    magnitude_sums = jnp.sum(grad_out.astype(f32) * pre_scale.astype(f32), axis=0)
    column_sums, magnitude_sums = lax.psum((column_sums, magnitude_sums), "dp")
    col_norm = jnp.sqrt(column_sums + 1e-06)
    scaled = (gathered.astype(f32) * (magnitude / col_norm)).astype(bf16)
    partial_value = jnp.einsum("tf,rf->tr", scaled, merged, preferred_element_type=f32)
    exchanged = lax.all_to_all(
        partial_value.astype(bf16), "dp", split_axis=0, concat_axis=1, tiled=True
    )
    grad_inputs = lax.psum_scatter(exchanged, "tensor", scatter_dimension=1, tiled=True)
    own_scaled = lax.dynamic_slice_in_dim(scaled, dp * tokens, tokens, 0)
    back_low = lax.psum(
        jnp.einsum(
            "tf,rf->tr", own_scaled, output_adapter_factor, preferred_element_type=f32
        ).astype(bf16),
        "tensor",
    )
    input_gradient = lax.psum(
        adapter_scale_factor
        * jnp.einsum("td,tr->dr", inputs, back_low, preferred_element_type=f32),
        "dp",
    )
    output_gradient = adapter_scale_factor * jnp.einsum(
        "tr,tf->rf", hidden_all, scaled, preferred_element_type=f32
    )
    return (grad_inputs, input_gradient, output_gradient, magnitude_sums / col_norm)


def solution(mesh):
    in_specs = (
        P("dp", "tensor"),
        P("dp", "tensor"),
        P(),
        P(None, "tensor"),
        P("tensor"),
        P("dp", "tensor"),
        P("dp", "tensor"),
        P("dp", "tensor"),
    )
    out_specs = (P("dp", "tensor"), P("tensor", None), P(None, "tensor"), P("tensor"))
    return jax.shard_map(
        on_device, mesh=mesh, in_specs=in_specs, out_specs=out_specs, check_vma=False
    )
```

time: 311 us -> 217 us (0.70)
  waiting for transfers between devices: 197 us -> 95.7 us
  blocking collectives: 39.5 us -> 49.1 us
  starting transfers between devices: 0.12 us -> 4.55 us
  other arithmetic: 12.2 us -> 8.8 us
    all_gather x1, waiting for transfers between devices: 140 us -> 21.2 us  [on_device(): gathered = lax.all_gather(grad_out, 'dp', axis=0, tiled=True)]
    psum x1, waiting for transfers between devices: 19 us -> 36.3 us  [on_device(): lax.psum(adapter_scale_factor * jnp.einsum('td,tr->dr', inputs, back_low,...]
    reduce_sum x2 -> x1, other arithmetic: 12.2 us -> 1.73 us  [on_device(): jnp.sum(grad_out.astype(f32) * pre_scale.astype(f32), axis=0)]
    all_gather x0 -> x1, blocking collectives: none -> 9.35 us  [on_device(): hidden_all = lax.all_gather(hidden_low, 'dp', axis=0, tiled=True)]
    convert_element_type x0 -> x1, other arithmetic: none -> 6.44 us  [on_device(): scaled = (gathered.astype(f32) * (magnitude / col_norm)).astype(bf16)]
    all_to_all x0 -> x1, starting transfers between devices: none -> 4.47 us  [on_device(): lax.all_to_all(partial_value.astype(bf16), 'dp', split_axis=0, concat_axi...]
  transfers between devices with their start and end apart: 3 -> 4, of which waited for: 3 -> 4; matrix products, arithmetic and copies ran while one was open for 6% -> 17% of each run, Pallas kernels for 0% -> 0%
where the time goes in v1:
time: 217 us; the launch traced here: 214 us
  waiting for transfers between devices  95.7 us (44%)
  blocking collectives  49.1 us (23%)
  matrix products  24.9 us (11%)
  local copies, waits for them, and re-layouts  16.9 us (8%)
  between operations  13.8 us (6%)
  other arithmetic  8.8 us (4%)
  starting transfers between devices  4.55 us (2%)
    reduce_scatter x1, waiting for transfers between devices, on_device(): lax.psum_scatter(exchanged, 'tensor', scatter_dimension=1, tiled=True)  37.2 us
    psum x1, waiting for transfers between devices, on_device(): lax.psum(adapter_scale_factor * jnp.einsum('td,tr->dr', inputs, back_low,...  36.3 us
    psum x1, blocking collectives, on_device(): column_sums, magnitude_sums = lax.psum((column_sums, magnitude_sums), 'dp')  23.7 us
    all_gather x1, waiting for transfers between devices, on_device(): gathered = lax.all_gather(grad_out, 'dp', axis=0, tiled=True)  21.2 us
    psum x1, blocking collectives, on_device(): lax.psum(jnp.einsum('tf,rf->tr', own_scaled, output_adapter_factor, prefe...  16.1 us
    all_gather x1, blocking collectives, on_device(): hidden_all = lax.all_gather(hidden_low, 'dp', axis=0, tiled=True)  9.35 us
    reshape x1, local copies, waits for them, and re-layouts, on_device(): expanded = jnp.repeat(block_scales, block_size, axis=1)  8.68 us
    dot_general x1, matrix products, on_device(): jnp.dot(adapter_row_block, output_adapter_factor, preferred_element_type=...  7.64 us
  transfers between devices with their start and end apart: 4, of which 4 were waited for; matrix products, arithmetic and copies ran while one was open for 17% of the time, Pallas kernels for 0%

profile of v1, /device:TPU:12, one launch (start us, length us, event | category | flops | bytes accessed | tf_op | source)
XLA Modules:
  0.0 213.8 jit_solution(14048464834680032486)
XLA Ops:
  7.2 0.0 copy-start
  7.2 0.0 all-gather.3.cloned.1.call-start
  7.2 0.7 all-gather.3.cloned.1.call-update
  7.9 4.8 %broadcast_in_dim.4 = f32[512,56,64]{0,2,1:T(8,128)} broadcast(f32[512,56]{0,1:T(8,128)} %param.9), dimensions={0,1} | broadcast | bytes 7454720 | tf_op jit(solution)/shard_map/broadcast_in_dim | solution.py:33
  12.7 0.0 copy-start.2
  12.7 0.0 copy-start.4
  12.7 8.7 %copy.17 = f32[512,3584]{1,0:T(8,128)} copy(f32[512,3584]{0,1:T(8,128)} %bitcast.21) | data formatting | bytes 14680064 | tf_op jit(solution)/shard_map/reshape | solution.py:33
  21.4 0.0 copy-done.2
  21.4 1.7 multiply_reduce_fusion.1
  23.1 0.0 copy-done
  23.2 0.0 copy-done.4
  23.2 0.0 copy-start.6
  23.2 7.6 %multiply_reduce_fusion = (f32[3584]{0:T(1024)S(1)}, bf16[512,3584]{1,0:T(8,128)(2,1)}) fusion(bf16[64,3584]{1,0:T(8,128)(2,1)S(1)} %copy-done.4, bf16[4096,64]{0,1:T(8,128)(2,1)S(1)} %copy-done, s32[]{:T(128)S(6)} %select_n.9, f32[512,3584]{1,0:T(8,128)} %copy.17, s32[512,3584]{1,0:T(8,128)} %param.8), kind=kOutput, calls=%fused_computation.1 | convolution fusion | flops 251392512 | bytes 18888708 | tf_op jit(solution)/shard_map/dot_general | solution.py:40
  30.8 23.7 %all-reduce = (f32[3584]{0:T(1024)S(1)}, f32[3584]{0:T(1024)S(1)}) all-reduce(f32[3584]{0:T(1024)S(1)} %get-tuple-element.10, f32[3584]{0:T(1024)S(1)} %multiply_reduce_fusion.1), channel_id=1, replica_groups=mesh['dp'=8,'tensor'=4] {'dp'}, use_global_device_ids=true, to_apply=%region_1.0 | all-reduce | flops 7168 | bytes 57344 | tf_op jit(solution)/shard_map/psum | solution.py:45
  54.5 0.0 copy-done.6
  54.5 0.6 fusion.9
  55.1 21.2 %all-gather.3.cloned.1.call-done = bf16[1536,3584]{1,0:T(8,128)(2,1)} async-done(((bf16[192,3584]{1,0:T(8,128)(2,1)}), bf16[1536,3584]{1,0:T(8,128)(2,1)}) %all-gather.3.cloned.1.call-update) | async-done | bytes 11010064 | tf_op jit(solution)/shard_map/all_gather | solution.py:24
  76.3 0.0 copy-start.3
  76.3 6.4 %multiply_convert_fusion = bf16[1536,3584]{1,0:T(8,128)(2,1)S(1)} fusion(bf16[1536,3584]{1,0:T(8,128)(2,1)} %all-gather.3.cloned.1.call-done, f32[3584]{0:T(1024)S(1)} %get-tuple-element.9), kind=kLoop, calls=%fused_computation | loop fusion | flops 16515072 | bytes 22034432 | tf_op jit(solution)/shard_map/convert_element_type | solution.py:47
  82.8 0.0 copy-start.1
  82.8 0.0 copy-done.3
  82.8 0.0 copy-start.5
  82.8 7.1 %convolution_convert_fusion = bf16[1536,512]{1,0:T(8,128)(2,1)} fusion(bf16[1536,3584]{1,0:T(8,128)(2,1)S(1)} %multiply_convert_fusion, bf16[512,3584]{1,0:T(8,128)(2,1)S(1)} %copy-done.3), kind=kOutput, calls=%fused_computation.4 | convolution fusion | flops 5637931008 | bytes 16252928 | tf_op jit(solution)/shard_map/tf,rf->tr/dot_general | solution.py:48
  89.9 0.0 copy-done.1
  89.9 4.5 %all-to-all-start = ((bf16[8,192,512]{2,1,0:T(8,128)(2,1)}), bf16[8,192,512]{2,1,0:T(8,128)(2,1)S(1)}, u32[]{:S(2)}, u32[]{:S(2)}) async-start(bf16[8,192,512]{2,1,0:T(8,128)(2,1)} %bitcast.24), calls=%async_computation | async-start | bytes 3145728 | tf_op jit(solution)/shard_map/all_to_all | solution.py:49
  94.4 0.0 all-reduce.4.cloned.1.call-start
  94.4 0.0 copy-done.5
  94.4 0.3 fusion.6
  94.6 1.9 fusion.3
  96.5 16.1 %all-reduce.1 = (bf16[192,64]{0,1:T(8,128)(2,1)S(1)}, bf16[192,64]{0,1:T(8,128)(2,1)S(1)}) all-reduce(bf16[192,64]{0,1:T(8,128)(2,1)S(1)} %fusion.3, bf16[192,64]{0,1:T(8,128)(2,1)S(1)} %fusion.6), channel_id=1, replica_groups=mesh['dp'=8,'tensor'=4] {'tensor'}, use_global_device_ids=true, to_apply=%region_3.0 | all-reduce | flops 24576 | bytes 98304 | tf_op jit(solution)/shard_map/psum | solution.py:54
  112.6 0.9 fusion.2
  113.5 0.0 all-reduce.4.cloned.1.call-update
  113.5 0.0 reduce-scatter.2.cloned.1.call-start
  113.6 0.3 all-to-all-done
  113.9 1.3 copy.20
  115.3 0.0 reduce-scatter.2.cloned.1.call-update
  115.3 9.3 %all-gather = bf16[8,192,64]{1,2,0:T(8,128)(2,1)S(1)} all-gather(bf16[1,192,64]{1,2,0:T(8,128)(2,1)S(1)} %bitcast.25), channel_id=1, replica_groups=mesh['dp'=8,'tensor'=4] {'dp'}, dimensions={0}, use_global_device_ids=true | all-gather | bytes 221184 | tf_op jit(solution)/shard_map/all_gather | solution.py:32
  124.6 0.1 copy.19
  124.8 0.2 reshape.17
  125.0 7.1 %convolution_multiply_fusion = f32[64,3584]{1,0:T(8,128)} fusion(bf16[1536,64]{0,1:T(8,128)(2,1)S(1)} %reshape.17, bf16[1536,3584]{1,0:T(8,128)(2,1)} %copy-done.1), kind=kOutput, calls=%fused_computation.3 | convolution fusion | flops 704872448 | bytes 12124160 | tf_op jit(solution)/shard_map/tr,tf->rf/dot_general | solution.py:65
  132.1 36.3 %all-reduce.4.cloned.1.call-done = f32[1024,64]{0,1:T(8,128)} async-done(((f32[1024,64]{0,1:T(8,128)}), f32[1024,64]{0,1:T(8,128)}) %all-reduce.4.cloned.1.call-update) | async-done | bytes 262160 | tf_op jit(solution)/shard_map/psum | solution.py:60
  168.4 37.2 %reduce-scatter.2.cloned.1.call-done = bf16[192,1024]{1,0:T(8,128)(2,1)} async-done(((bf16[192,4096]{1,0:T(8,128)(2,1)}), bf16[192,1024]{1,0:T(8,128)(2,1)}) %reduce-scatter.2.cloned.1.call-update) | async-done | bytes 393232 | tf_op jit(solution)/shard_map/reduce_scatter | solution.py:52
  205.6 1.7 copy.22
Async XLA Ops:
  7.2 16.0 %copy-start = (bf16[4096,64]{0,1:T(8,128)(2,1)S(1)}, bf16[4096,64]{0,1:T(8,128)(2,1)}, u32[]{:S(2)}) copy-start(bf16[4096,64]{0,1:T(8,128)(2,1)} %param.10) | copy-start | bytes 1572868
  7.2 69.1 %all-gather.3.cloned.1.call-start = ((), (), s32[]{:S(2)}) async-start(), calls=%async_computation.2 | async-start | bytes 12386304 | tf_op jit(solution)/shard_map/all_gather | solution.py:24
  12.7 8.7 %copy-start.2 = (bf16[192,3584]{1,0:T(8,128)(2,1)S(1)}, bf16[192,3584]{1,0:T(8,128)(2,1)}, u32[]{:S(2)}) copy-start(bf16[192,3584]{1,0:T(8,128)(2,1)} %param.14) | copy-start | bytes 4128772
  12.7 10.4 %copy-start.4 = (bf16[64,3584]{1,0:T(8,128)(2,1)S(1)}, bf16[64,3584]{1,0:T(8,128)(2,1)}, u32[]{:S(2)}) copy-start(bf16[64,3584]{1,0:T(8,128)(2,1)} %param.11) | copy-start | bytes 1376260
  23.2 31.3 %copy-start.6 = (f32[3584]{0:T(1024)S(1)}, f32[3584]{0:T(1024)}, u32[]{:S(2)}) copy-start(f32[3584]{0:T(1024)} %param.12) | copy-start | bytes 43012
  76.3 6.5 %copy-start.3 = (bf16[512,3584]{1,0:T(8,128)(2,1)S(1)}, bf16[512,3584]{1,0:T(8,128)(2,1)}, u32[]{:S(2)}) copy-start(bf16[512,3584]{1,0:T(8,128)(2,1)} %get-tuple-element.11) | copy-start | bytes 11010052
  82.8 7.1 %copy-start.1 = (bf16[1536,3584]{1,0:T(8,128)(2,1)}, bf16[1536,3584]{1,0:T(8,128)(2,1)S(1)}, u32[]{:S(2)}) copy-start(bf16[1536,3584]{1,0:T(8,128)(2,1)S(1)} %multiply_convert_fusion) | copy-start | bytes 33030148
  82.8 11.6 %copy-start.5 = (bf16[192,1024]{1,0:T(8,128)(2,1)S(1)}, bf16[192,1024]{1,0:T(8,128)(2,1)}, u32[]{:S(2)}) copy-start(bf16[192,1024]{1,0:T(8,128)(2,1)} %param.13) | copy-start | bytes 1179652
  89.9 24.0 %all-to-all-start = ((bf16[8,192,512]{2,1,0:T(8,128)(2,1)}), bf16[8,192,512]{2,1,0:T(8,128)(2,1)S(1)}, u32[]{:S(2)}, u32[]{:S(2)}) async-start(bf16[8,192,512]{2,1,0:T(8,128)(2,1)} %bitcast.24), calls=%async_computation | async-start | bytes 3145728 | tf_op jit(solution)/shard_map/all_to_all | solution.py:49
  94.4 74.0 %all-reduce.4.cloned.1.call-start = ((), (), s32[]{:S(2)}) async-start(), calls=%async_computation.4 | async-start | bytes 524288 | tf_op jit(solution)/shard_map/psum | solution.py:60
  113.5 92.1 %reduce-scatter.2.cloned.1.call-start = ((), (), s32[]{:S(2)}) async-start(), calls=%async_computation.3 | async-start | bytes 1966080 | tf_op jit(solution)/shard_map/reduce_scatter | solution.py:52
Sparse Core Ops, SparseCore 0:
  9.9 66.3 all-gather.2
  113.7 54.6 all-reduce.3
  171.4 34.2 reduce-scatter.1

commit v2 on v1

--- a/solution.py
+++ b/solution.py
@@ -1,6 +1,8 @@
 import jax
 import jax.numpy as jnp
 from jax import lax
+from jax.experimental import pallas as pl
+from jax.experimental.pallas import tpu as pltpu
 from jax.sharding import PartitionSpec as P
 
 adapter_scale_factor = 0.5
@@ -68,7 +70,410 @@
     return (grad_inputs, input_gradient, output_gradient, magnitude_sums / col_norm)
 
 
+MESH = pl.DeviceIdType.MESH
+COLUMN_TILE = 512
+
+
+def flip(bit, by):
+    return bit + by - 2 * bit * by
+
+
+def fused_kernel(
+    codes_hbm,
+    scales_ref,
+    first_ref,
+    second_ref,
+    magnitude_ref,
+    inputs_ref,
+    grad_hbm,
+    pre_hbm,
+    out_ref,
+    first_out,
+    second_out,
+    magnitude_out,
+    codes,
+    pre,
+    tokens,
+    weight,
+    stats,
+    factor,
+    low_parts,
+    low,
+    back_parts,
+    back_acc,
+    acc,
+    product,
+    returned,
+    across,
+    second_parts,
+    second_pair,
+    first_split,
+    first_recv,
+    first_full,
+    local_sem,
+    send_sem,
+    recv_sem,
+):
+    f32, bf16 = jnp.float32, jnp.bfloat16
+    rows, width = codes.shape
+    count = tokens.shape[1]
+    half = count // 2
+    tile = COLUMN_TILE
+    steps = width // tile
+    rank = low.shape[2]
+    block = width // scales_ref.shape[1]
+    dp, z = lax.axis_index("dp"), lax.axis_index("tensor")
+    core = lax.rem(dp, 2)
+    x = lax.rem(dp // 2, 2)
+    y = dp // 4
+    z_low, z_high = lax.rem(z, 2), z // 2
+
+    def plane(offset):
+        return (
+            flip(y, offset // 4) * 4 + flip(x, (offset // 2) % 2) * 2 + flip(core, offset % 2)
+        )
+
+    def stack(offset):
+        return flip(z_high, offset // 2) * 2 + flip(z_low, offset % 2)
+
+    used = [0]
+    sent = []
+
+    def remote(source, target, to, start=True):
+        index = used[0]
+        used[0] += 1
+        copy = pltpu.make_async_remote_copy(
+            src_ref=source,
+            dst_ref=target,
+            send_sem=send_sem.at[index],
+            recv_sem=recv_sem.at[index],
+            device_id=to,
+            device_id_type=MESH,
+        )
+        copy.start()
+        sent.append(copy)
+        return copy
+
+    def arrival(source, target, copy_index, to):
+        return pltpu.make_async_remote_copy(
+            src_ref=source,
+            dst_ref=target,
+            send_sem=send_sem.at[copy_index],
+            recv_sem=recv_sem.at[copy_index],
+            device_id=to,
+            device_id_type=MESH,
+        )
+
+    def peer(offset):
+        return {"dp": plane(offset), "tensor": z}
+
+    def over(offset):
+        return {"dp": dp, "tensor": stack(offset)}
+
+    codes_copy = pltpu.make_async_copy(codes_hbm, codes, local_sem.at[0])
+    pre_copy = pltpu.make_async_copy(pre_hbm, pre, local_sem.at[1])
+    own_copy = pltpu.make_async_copy(grad_hbm, tokens.at[0], local_sem.at[2])
+    codes_copy.start()
+    pre_copy.start()
+    own_copy.start()
+
+    barrier = pltpu.get_barrier_semaphore()
+    for offset in range(1, 8):
+        pl.semaphore_signal(barrier, inc=1, device_id=peer(offset), device_id_type=MESH)
+    for offset in range(1, 4):
+        pl.semaphore_signal(barrier, inc=1, device_id=over(offset), device_id_type=MESH)
+    pl.semaphore_wait(barrier, 10)
+
+    lower, upper = pl.ds(0, half), pl.ds(half, half)
+    from_x = [
+        remote(grad_hbm.at[lower], tokens.at[1, lower], peer(2)),
+    ]
+    from_y = [
+        remote(grad_hbm.at[upper], tokens.at[2, upper], peer(4)),
+    ]
+    from_x.append(remote(grad_hbm.at[upper], tokens.at[1, upper], peer(2)))
+    from_y.append(remote(grad_hbm.at[lower], tokens.at[2, lower], peer(4)))
+
+    depth = inputs_ref.shape[1]
+    low_parts[0] = jnp.dot(
+        inputs_ref[...],
+        first_ref[pl.ds(pl.multiple_of(z * depth, depth), depth), :],
+        preferred_element_type=f32,
+    ).astype(bf16)
+    low_copies = [remote(low_parts.at[0], low_parts.at[r], over(r)) for r in range(1, 4)]
+
+    own_rows = pl.ds(pl.multiple_of(dp * rows, rows), rows)
+    codes_copy.wait()
+    pre_copy.wait()
+    own_copy.wait()
+
+    def dequantize(step, carry):
+        columns = pl.ds(pl.multiple_of(step * tile, tile), tile)
+        scales = scales_ref[...]
+        high = scales.astype(bf16)
+        rest = scales - high.astype(f32)
+        middle = rest.astype(bf16)
+        last = (rest - middle.astype(f32)).astype(bf16)
+        shape = (scales.shape[1], tile)
+        place = lax.broadcasted_iota(jnp.int32, shape, 1) // block + step * (tile // block)
+        spread = jnp.where(lax.broadcasted_iota(jnp.int32, shape, 0) == place, 1.0, 0.0).astype(bf16)
+        expanded = (
+            jnp.dot(high, spread, preferred_element_type=f32)
+            + jnp.dot(middle, spread, preferred_element_type=f32)
+            + jnp.dot(last, spread, preferred_element_type=f32)
+        )
+        adapter = jnp.dot(first_ref[own_rows, :], second_ref[:, columns], preferred_element_type=f32)
+        merged = (
+            (codes[:, columns].astype(f32) - 7.5) * expanded + adapter_scale_factor * adapter
+        ).astype(bf16)
+        weight[core, :, columns] = merged
+        merged_f = merged.astype(f32)
+        stats[0, 0:1, columns] = jnp.sum(merged_f * merged_f, axis=0, keepdims=True)
+        stats[0, 1:2, columns] = jnp.sum(
+            tokens[0, :, columns].astype(f32) * pre[:, columns].astype(f32), axis=0, keepdims=True
+        )
+        return carry
+
+    lax.fori_loop(0, steps, dequantize, 0)
+
+    stats_copies = [remote(stats.at[0], stats.at[o], peer(o)) for o in range(1, 8)]
+    weight_index = used[0]
+    remote(weight.at[core], weight.at[core], peer(1))
+    weight_arrival = arrival(weight.at[core], weight.at[1 - core], weight_index, peer(1))
+
+    for copy in low_copies:
+        copy.wait_recv()
+    low[0] = (
+        (low_parts[0].astype(f32) + low_parts[1].astype(f32))
+        + (low_parts[2].astype(f32) + low_parts[3].astype(f32))
+    ).astype(bf16)
+    plane_low = [remote(low.at[0], low.at[b], peer(2 * b)) for b in range(1, 4)]
+
+    from_x[0].wait_recv()
+    far_lower = remote(tokens.at[1, lower], tokens.at[3, lower], peer(4))
+    from_y[0].wait_recv()
+    far_upper = remote(tokens.at[2, upper], tokens.at[3, upper], peer(2))
+
+    for copy in stats_copies:
+        copy.wait_recv()
+    total = ((stats[0] + stats[1]) + (stats[2] + stats[3])) + (
+        (stats[4] + stats[5]) + (stats[6] + stats[7])
+    )
+    norm = jnp.sqrt(total[0:1, :] + 1e-06)
+    factor[...] = magnitude_ref[...] / norm
+    magnitude_out[...] = total[1:2, :] / norm
+
+    weight_arrival.wait_recv()
+
+    across_sends = []
+    across_index = used[0]
+    used[0] += 8
+
+    def across_copy(which, source, target_slot, to_z):
+        return pltpu.make_async_remote_copy(
+            src_ref=source,
+            dst_ref=across.at[target_slot],
+            send_sem=send_sem.at[across_index + which],
+            recv_sem=recv_sem.at[across_index + target_slot],
+            device_id={"dp": dp, "tensor": to_z},
+            device_id_type=MESH,
+        )
+
+    def send_across(which):
+        quarter_high, quarter_low = flip(y, which // 2), flip(x, which % 2)
+        to_z = quarter_high * 2 + quarter_low
+        slot = flip(quarter_high, z_high) * 2 + flip(quarter_low, z_low)
+        copy = across_copy(which, returned.at[which], slot, to_z)
+
+        @pl.when(to_z != z)
+        def _():
+            copy.start()
+
+        across_sends.append((copy, to_z))
+
+    nt = (((1,), (1,)), ((), ()))
+    tn = (((0,), (0,)), ((), ()))
+
+    def multiply(which, destination):
+        acc[...] = jnp.zeros_like(acc)
+        if which == 0:
+            back_acc[...] = jnp.zeros_like(back_acc)
+
+        def body(step, carry):
+            columns = pl.ds(pl.multiple_of(step * tile, tile), tile)
+            scaled = (tokens[which, :, columns].astype(f32) * factor[:, columns]).astype(bf16)
+            for side in range(2):
+                acc[side] += lax.dot_general(
+                    scaled, weight[side, :, columns], nt, preferred_element_type=f32
+                )
+            second_parts[which, :, columns] = lax.dot_general(
+                low[which], scaled, tn, preferred_element_type=f32
+            )
+            if which == 0:
+                back_acc[...] += lax.dot_general(
+                    scaled, second_ref[:, columns], nt, preferred_element_type=f32
+                )
+            return carry
+
+        lax.fori_loop(0, steps, body, 0)
+        for side in range(2):
+            destination[:, pl.ds(side * rows, rows)] = acc[side].astype(bf16)
+
+    multiply(0, returned.at[0])
+    send_across(0)
+    back_parts[0] = back_acc[...].astype(bf16)
+    back_copies = [remote(back_parts.at[0], back_parts.at[r], over(r)) for r in range(1, 4)]
+
+    returns = {}
+    from_x[1].wait_recv()
+    plane_low[0].wait_recv()
+    multiply(1, product.at[0])
+    returns[1] = remote(product.at[0], returned.at[1], peer(2))
+
+    for copy in back_copies:
+        copy.wait_recv()
+    back = (
+        (back_parts[0].astype(f32) + back_parts[1].astype(f32))
+        + (back_parts[2].astype(f32) + back_parts[3].astype(f32))
+    ).astype(bf16)
+    slices = first_split.shape[0]
+    piece = rank // slices
+    gradient = adapter_scale_factor * lax.dot_general(
+        back, inputs_ref[...], tn, preferred_element_type=f32
+    )
+    for index in range(slices):
+        first_split[index] = gradient[index * piece : (index + 1) * piece, :]
+    first_copies = [
+        remote(first_split.at[plane(o)], first_recv.at[o], peer(o)) for o in range(1, 8)
+    ]
+
+    from_y[1].wait_recv()
+    plane_low[1].wait_recv()
+    multiply(2, product.at[1])
+    returns[2] = remote(product.at[1], returned.at[2], peer(4))
+
+    for copy in first_copies:
+        copy.wait_recv()
+    first_recv[0] = first_split[dp]
+    first_full[dp] = (
+        (first_recv[0] + first_recv[1]) + (first_recv[2] + first_recv[3])
+    ) + ((first_recv[4] + first_recv[5]) + (first_recv[6] + first_recv[7]))
+    first_index = used[0]
+    for o in range(1, 8):
+        remote(first_full.at[dp], first_full.at[dp], peer(o))
+
+    returns[1].wait_recv()
+    send_across(1)
+    returns[2].wait_recv()
+    send_across(2)
+
+    far_lower.wait_recv()
+    far_upper.wait_recv()
+    plane_low[2].wait_recv()
+    multiply(3, product.at[2])
+    returns[3] = remote(product.at[2], returned.at[3], peer(6))
+
+    second_pair[0] = (second_parts[0] + second_parts[1]) + (second_parts[2] + second_parts[3])
+    pair_copy = remote(second_pair.at[0], second_pair.at[1], peer(1))
+
+    for o in range(1, 8):
+        arrival(
+            first_full.at[dp], first_full.at[plane(o)], first_index + o - 1, peer(o)
+        ).wait_recv()
+    first_out[...] = jnp.transpose(first_full[...].reshape(rank, depth))
+
+    returns[3].wait_recv()
+    send_across(3)
+
+    pair_copy.wait_recv()
+    second_out[...] = adapter_scale_factor * (second_pair[0] + second_pair[1])
+
+    for slot in range(1, 4):
+        across_copy(slot, returned.at[slot], slot, stack(slot)).wait_recv()
+    mine = flip(z_high, y) * 2 + flip(z_low, x)
+    out_ref[...] = (
+        (returned[mine].astype(f32) + across[1].astype(f32))
+        + (across[2].astype(f32) + across[3].astype(f32))
+    ).astype(bf16)
+
+    for copy in sent:
+        copy.wait_send()
+    for copy, to_z in across_sends:
+
+        @pl.when(to_z != z)
+        def _(copy=copy):
+            copy.wait_send()
+
+
+def on_device_fused(
+    base_codes,
+    block_scales,
+    input_adapter_factor,
+    output_adapter_factor,
+    magnitude,
+    inputs,
+    grad_out,
+    pre_scale,
+):
+    f32, bf16 = jnp.float32, jnp.bfloat16
+    rows, width = base_codes.shape
+    count, depth = inputs.shape
+    rank = input_adapter_factor.shape[1]
+    whole = pl.BlockSpec(memory_space=pltpu.VMEM)
+    away = pl.BlockSpec(memory_space=pl.ANY)
+    grad_inputs, first, second, grad_magnitude = pl.pallas_call(
+        fused_kernel,
+        out_shape=(
+            jax.ShapeDtypeStruct((count, depth), bf16),
+            jax.ShapeDtypeStruct((depth, rank), f32),
+            jax.ShapeDtypeStruct((rank, width), f32),
+            jax.ShapeDtypeStruct((1, width), f32),
+        ),
+        in_specs=[away, whole, whole, whole, whole, whole, away, away],
+        out_specs=(whole, whole, whole, whole),
+        scratch_shapes=[
+            pltpu.VMEM((rows, width), jnp.int32),
+            pltpu.VMEM((count, width), bf16),
+            pltpu.VMEM((4, count, width), bf16),
+            pltpu.VMEM((2, rows, width), bf16),
+            pltpu.VMEM((8, 2, width), f32),
+            pltpu.VMEM((1, width), f32),
+            pltpu.VMEM((4, count, rank), bf16),
+            pltpu.VMEM((4, count, rank), bf16),
+            pltpu.VMEM((4, count, rank), bf16),
+            pltpu.VMEM((count, rank), f32),
+            pltpu.VMEM((2, count, rows), f32),
+            pltpu.VMEM((3, count, depth), bf16),
+            pltpu.VMEM((4, count, depth), bf16),
+            pltpu.VMEM((4, count, depth), bf16),
+            pltpu.VMEM((4, rank, width), f32),
+            pltpu.VMEM((2, rank, width), f32),
+            pltpu.VMEM((8, rank // 8, depth), f32),
+            pltpu.VMEM((8, rank // 8, depth), f32),
+            pltpu.VMEM((8, rank // 8, depth), f32),
+            pltpu.SemaphoreType.DMA((3,)),
+            pltpu.SemaphoreType.DMA((64,)),
+            pltpu.SemaphoreType.DMA((64,)),
+        ],
+        compiler_params=pltpu.CompilerParams(
+            collective_id=0, has_side_effects=True, vmem_limit_bytes=58 * 1024 * 1024
+        ),
+    )(
+        base_codes,
+        block_scales,
+        input_adapter_factor,
+        output_adapter_factor,
+        magnitude.reshape(1, width),
+        inputs,
+        grad_out,
+        pre_scale,
+    )
+    return grad_inputs, first, second, grad_magnitude.reshape(width)
+
+
 def solution(mesh):
+    fits = mesh.shape["dp"] == 8 and mesh.shape["tensor"] == 4
+    body = on_device_fused if fits else on_device
     in_specs = (
         P("dp", "tensor"),
         P("dp", "tensor"),
@@ -81,5 +486,5 @@
     )
     out_specs = (P("dp", "tensor"), P("tensor", None), P(None, "tensor"), P("tensor"))
     return jax.shard_map(
-        on_device, mesh=mesh, in_specs=in_specs, out_specs=out_specs, check_vma=False
-    )
+        body, mesh=mesh, in_specs=in_specs, out_specs=out_specs, check_vma=False
+    )

time: 217 us -> 138 us (0.64); the launches traced: 214 us -> 137 us
  Pallas kernels: 0 us -> 125 us
  waiting for transfers between devices: 95.7 us -> 0 us
  blocking collectives: 49.1 us -> 0 us
  matrix products: 24.9 us -> 0 us
  between operations: 13.8 us -> 0.65 us
  other arithmetic: 8.8 us -> 1.44 us
  local copies, waits for them, and re-layouts: 16.9 us -> 10.1 us
  starting transfers between devices: 4.55 us -> 0 us
    pallas_call x0 -> x1, Pallas kernels: none -> 125 us  [on_device_fused(): pl.pallas_call(fused_kernel, out_shape=(jax.ShapeDtypeStruct((count, dept...]
    psum x2 -> x0, blocking collectives: 39.8 us -> none  [the longest x1 23.7 us: on_device(): column_sums, magnitude_sums = lax.psum((column_sums, magnitude_sums), 'dp')]
    reduce_scatter x1 -> x0, waiting for transfers between devices: 37.2 us -> none  [on_device(): lax.psum_scatter(exchanged, 'tensor', scatter_dimension=1, tiled=True)]
    psum x1 -> x0, waiting for transfers between devices: 36.3 us -> none  [on_device(): lax.psum(adapter_scale_factor * jnp.einsum('td,tr->dr', inputs, back_low,...]
    dot_general x6 -> x0, matrix products: 24.9 us -> none  [the longest x1 7.64 us: on_device(): jnp.dot(adapter_row_block, output_adapter_factor, preferred_element_type=...]
    all_gather x1 -> x0, waiting for transfers between devices: 21.2 us -> none  [on_device(): gathered = lax.all_gather(grad_out, 'dp', axis=0, tiled=True)]
    all_gather x1 -> x0, blocking collectives: 9.35 us -> none  [on_device(): hidden_all = lax.all_gather(hidden_low, 'dp', axis=0, tiled=True)]
    reshape x1, local copies, waits for them, and re-layouts: 8.68 us -> 1.33 us  [on_device_fused(): magnitude.reshape(1, width)]
  transfers between devices with their start and end apart: 4 -> 0, of which waited for: 4 -> 0; matrix products, arithmetic and copies ran while one was open for 17% -> 0% of each run, Pallas kernels for 0% -> 0%
where the time goes in v2:
time: 138 us; the launch traced here: 137 us
  Pallas kernels  125 us (91%)
  local copies, waits for them, and re-layouts  10.1 us (7%)
  other arithmetic  1.44 us (1%)
    pallas_call x1, Pallas kernels, on_device_fused(): pl.pallas_call(fused_kernel, out_shape=(jax.ShapeDtypeStruct((count, dept...  125 us
    unnamed x7, local copies, waits for them, and re-layouts  8.73 us

profile of v2, /device:TPU:12, one launch (start us, length us, event | category | flops | bytes accessed | tf_op | source)
XLA Modules:
  0.0 137.2 jit_solution(6903896802681296125)
XLA Ops:
  0.6 1.3 reshape.14.magnitude_ref
  2.0 1.7 %copy.12.scales_ref = f32[512,56]{1,0:T(8,128)} copy(f32[512,56]{0,1:T(8,128)} %param.9) | data formatting | bytes 229376 | tf_op args[1]
  3.7 2.4 %copy.13.first_ref = bf16[4096,64]{1,0:T(8,128)(2,1)} copy(bf16[4096,64]{0,1:T(8,128)(2,1)} %param.10) | data formatting | bytes 1048576 | tf_op args[2]
  6.1 125.0 %shard_map.111 = (bf16[192,1024]{1,0:T(8,128)(2,1)}, f32[1024,64]{1,0:T(8,128)}, f32[64,3584]{1,0:T(8,128)}, f32[1,3584]{1,0:T(1,128)}) custom-call(s32[512,3584]{1,0:T(8,128)} %codes_hbm.1, f32[512,56]{1,0:T(8,128)} %copy.12.scales_ref, bf16[4096,64]{1,0:T(8,128)(2,1)} %copy.13.first_ref, bf16[64,3584]{1,0:T(8,128)(2,1)} %second_ref.1, ...), custom_call_target="tpu_custom_call" | custom-call | tf_op jit(solution)/shard_map/pallas_call | solution.py:424
  131.1 0.0 copy-start
  131.1 1.4 %reduce = f32[3584]{0:T(1024)} reduce(f32[1,3584]{1,0:T(1,128)} %get-tuple-element.11, f32[]{:T(128)} %constant), dimensions={0}, to_apply=%get-tuple-element.11.reduce_sub_computation | reduce | bytes 28676 | tf_op jit(solution)/shard_map/pallas_call | solution.py:424
  132.6 1.9 %copy.14 = f32[1024,64]{0,1:T(8,128)} copy(f32[1024,64]{1,0:T(8,128)} %get-tuple-element.13) | data formatting | bytes 524288
  134.5 1.8 %copy.17 = bf16[192,1024]{1,0:T(8,128)(2,1)} copy(bf16[192,1024]{1,0:T(8,128)(2,1)} %get-tuple-element.20) | data formatting | bytes 786432
  136.3 0.0 copy-done
  136.3 0.9 copy.18
Async XLA Ops:
  131.1 5.1 %copy-start = (f32[64,3584]{1,0:T(8,128)S(1)}, f32[64,3584]{1,0:T(8,128)}, u32[]{:S(2)}) copy-start(f32[64,3584]{1,0:T(8,128)} %get-tuple-element.22) | copy-start | bytes 2752516

commit v3 on v2

--- a/solution.py
+++ b/solution.py
@@ -104,9 +104,11 @@
     acc,
     product,
     returned,
-    across,
+    arriving,
     second_parts,
     second_pair,
+    pieces,
+    adapter_rows,
     first_split,
     first_recv,
     first_full,
@@ -121,7 +123,7 @@
     tile = COLUMN_TILE
     steps = width // tile
     rank = low.shape[2]
-    block = width // scales_ref.shape[1]
+    block = width // scales_ref.shape[0]
     dp, z = lax.axis_index("dp"), lax.axis_index("tensor")
     core = lax.rem(dp, 2)
     x = lax.rem(dp // 2, 2)
@@ -195,34 +197,40 @@
     from_y.append(remote(grad_hbm.at[lower], tokens.at[2, lower], peer(4)))
 
     depth = inputs_ref.shape[1]
-    low_parts[0] = jnp.dot(
+    nt = (((1,), (1,)), ((), ()))
+    tn = (((0,), (0,)), ((), ()))
+    low_parts[0] = lax.dot_general(
         inputs_ref[...],
-        first_ref[pl.ds(pl.multiple_of(z * depth, depth), depth), :],
+        first_ref[:, pl.ds(pl.multiple_of(z * depth, depth), depth)],
+        nt,
         preferred_element_type=f32,
     ).astype(bf16)
     low_copies = [remote(low_parts.at[0], low_parts.at[r], over(r)) for r in range(1, 4)]
 
     own_rows = pl.ds(pl.multiple_of(dp * rows, rows), rows)
+    adapter_rows[...] = jnp.transpose(first_ref[:, own_rows].astype(f32)).astype(bf16)
+    scales = jnp.transpose(scales_ref[...])
+    high = scales.astype(bf16)
+    rest = scales - high.astype(f32)
+    middle = rest.astype(bf16)
+    pieces[0] = high
+    pieces[1] = middle
+    pieces[2] = (rest - middle.astype(f32)).astype(bf16)
     codes_copy.wait()
     pre_copy.wait()
     own_copy.wait()
 
     def dequantize(step, carry):
         columns = pl.ds(pl.multiple_of(step * tile, tile), tile)
-        scales = scales_ref[...]
-        high = scales.astype(bf16)
-        rest = scales - high.astype(f32)
-        middle = rest.astype(bf16)
-        last = (rest - middle.astype(f32)).astype(bf16)
-        shape = (scales.shape[1], tile)
+        shape = (scales_ref.shape[0], tile)
         place = lax.broadcasted_iota(jnp.int32, shape, 1) // block + step * (tile // block)
         spread = jnp.where(lax.broadcasted_iota(jnp.int32, shape, 0) == place, 1.0, 0.0).astype(bf16)
         expanded = (
-            jnp.dot(high, spread, preferred_element_type=f32)
-            + jnp.dot(middle, spread, preferred_element_type=f32)
-            + jnp.dot(last, spread, preferred_element_type=f32)
+            jnp.dot(pieces[0], spread, preferred_element_type=f32)
+            + jnp.dot(pieces[1], spread, preferred_element_type=f32)
+            + jnp.dot(pieces[2], spread, preferred_element_type=f32)
         )
-        adapter = jnp.dot(first_ref[own_rows, :], second_ref[:, columns], preferred_element_type=f32)
+        adapter = jnp.dot(adapter_rows[...], second_ref[:, columns], preferred_element_type=f32)
         merged = (
             (codes[:, columns].astype(f32) - 7.5) * expanded + adapter_scale_factor * adapter
         ).astype(bf16)
@@ -260,55 +268,67 @@
         (stats[4] + stats[5]) + (stats[6] + stats[7])
     )
     norm = jnp.sqrt(total[0:1, :] + 1e-06)
-    factor[...] = magnitude_ref[...] / norm
-    magnitude_out[...] = total[1:2, :] / norm
+    factor[...] = magnitude_ref[...].reshape(1, width) / norm
+    magnitude_out[...] = (total[1:2, :] / norm).reshape(width)
 
     weight_arrival.wait_recv()
 
-    across_sends = []
-    across_index = used[0]
-    used[0] += 8
-
-    def across_copy(which, source, target_slot, to_z):
+    halves = (lower, upper)
+    chain_sends = []
+    chain_index = used[0]
+    used[0] += 16
+
+    def chain_copy(which, part, side, to_z):
         return pltpu.make_async_remote_copy(
-            src_ref=source,
-            dst_ref=across.at[target_slot],
-            send_sem=send_sem.at[across_index + which],
-            recv_sem=recv_sem.at[across_index + target_slot],
+            src_ref=returned.at[which, halves[part]],
+            dst_ref=arriving.at[side, which, halves[part]],
+            send_sem=send_sem.at[chain_index + which * 2 + part],
+            recv_sem=recv_sem.at[chain_index + (side * 4 + which) * 2 + part],
             device_id={"dp": dp, "tensor": to_z},
             device_id_type=MESH,
         )
 
-    def send_across(which):
-        quarter_high, quarter_low = flip(y, which // 2), flip(x, which % 2)
-        to_z = quarter_high * 2 + quarter_low
-        slot = flip(quarter_high, z_high) * 2 + flip(quarter_low, z_low)
-        copy = across_copy(which, returned.at[which], slot, to_z)
-
-        @pl.when(to_z != z)
-        def _():
-            copy.start()
-
-        across_sends.append((copy, to_z))
-
-    nt = (((1,), (1,)), ((), ()))
-    tn = (((0,), (0,)), ((), ()))
-
-    def multiply(which, destination):
-        acc[...] = jnp.zeros_like(acc)
+    def chain(which, part):
+        owner = flip(y, which // 2) * 2 + flip(x, which % 2)
+        for side in range(2):
+            toward, last = ((1, 0), (-1, 3))[side]
+            copy = chain_copy(which, part, side, lax.rem(z + toward + 4, 4))
+            active = z < owner if side == 0 else z > owner
+
+            @pl.when(active)
+            def _(copy=copy, side=side, last=last):
+                @pl.when(z != last)
+                def _():
+                    copy.wait_recv()
+                    returned[which, halves[part]] = (
+                        returned[which, halves[part]].astype(f32)
+                        + arriving[side, which, halves[part]].astype(f32)
+                    ).astype(bf16)
+
+                copy.start()
+
+            chain_sends.append((copy, active))
+
+    def multiply(which, destination, start, size, second):
+        part = pl.ds(start, size)
+        acc[:, part] = jnp.zeros((2, size, rows), f32)
         if which == 0:
             back_acc[...] = jnp.zeros_like(back_acc)
 
         def body(step, carry):
             columns = pl.ds(pl.multiple_of(step * tile, tile), tile)
-            scaled = (tokens[which, :, columns].astype(f32) * factor[:, columns]).astype(bf16)
+            if second:
+                scaled = (tokens[which, :, columns].astype(f32) * factor[:, columns]).astype(bf16)
+                second_parts[which, :, columns] = lax.dot_general(
+                    low[which], scaled, tn, preferred_element_type=f32
+                )
+                piece = scaled[start : start + size, :]
+            else:
+                piece = (tokens[which, part, columns].astype(f32) * factor[:, columns]).astype(bf16)
             for side in range(2):
-                acc[side] += lax.dot_general(
-                    scaled, weight[side, :, columns], nt, preferred_element_type=f32
+                acc[side, part] += lax.dot_general(
+                    piece, weight[side, :, columns], nt, preferred_element_type=f32
                 )
-            second_parts[which, :, columns] = lax.dot_general(
-                low[which], scaled, tn, preferred_element_type=f32
-            )
             if which == 0:
                 back_acc[...] += lax.dot_general(
                     scaled, second_ref[:, columns], nt, preferred_element_type=f32
@@ -317,18 +337,19 @@
 
         lax.fori_loop(0, steps, body, 0)
         for side in range(2):
-            destination[:, pl.ds(side * rows, rows)] = acc[side].astype(bf16)
-
-    multiply(0, returned.at[0])
-    send_across(0)
+            destination[part, pl.ds(side * rows, rows)] = acc[side, part].astype(bf16)
+
+    multiply(0, returned.at[0], 0, count, True)
     back_parts[0] = back_acc[...].astype(bf16)
     back_copies = [remote(back_parts.at[0], back_parts.at[r], over(r)) for r in range(1, 4)]
 
     returns = {}
     from_x[1].wait_recv()
     plane_low[0].wait_recv()
-    multiply(1, product.at[0])
+    multiply(1, product.at[0], 0, count, True)
     returns[1] = remote(product.at[0], returned.at[1], peer(2))
+    chain(0, 0)
+    chain(0, 1)
 
     for copy in back_copies:
         copy.wait_recv()
@@ -349,7 +370,7 @@
 
     from_y[1].wait_recv()
     plane_low[1].wait_recv()
-    multiply(2, product.at[1])
+    multiply(2, product.at[1], 0, count, True)
     returns[2] = remote(product.at[1], returned.at[2], peer(4))
 
     for copy in first_copies:
@@ -362,16 +383,25 @@
     for o in range(1, 8):
         remote(first_full.at[dp], first_full.at[dp], peer(o))
 
-    returns[1].wait_recv()
-    send_across(1)
-    returns[2].wait_recv()
-    send_across(2)
-
     far_lower.wait_recv()
+    multiply(3, product.at[2], 0, half, False)
+    far_returns = [remote(product.at[2, lower], returned.at[3, lower], peer(6))]
     far_upper.wait_recv()
     plane_low[2].wait_recv()
-    multiply(3, product.at[2])
-    returns[3] = remote(product.at[2], returned.at[3], peer(6))
+    multiply(3, product.at[2], half, half, True)
+    far_returns.append(remote(product.at[2, upper], returned.at[3, upper], peer(6)))
+
+    returns[1].wait_recv()
+    chain(1, 0)
+    chain(1, 1)
+    returns[2].wait_recv()
+    chain(2, 0)
+    chain(2, 1)
+
+    far_returns[0].wait_recv()
+    chain(3, 0)
+    far_returns[1].wait_recv()
+    chain(3, 1)
 
     second_pair[0] = (second_parts[0] + second_parts[1]) + (second_parts[2] + second_parts[3])
     pair_copy = remote(second_pair.at[0], second_pair.at[1], peer(1))
@@ -380,27 +410,36 @@
         arrival(
             first_full.at[dp], first_full.at[plane(o)], first_index + o - 1, peer(o)
         ).wait_recv()
-    first_out[...] = jnp.transpose(first_full[...].reshape(rank, depth))
-
-    returns[3].wait_recv()
-    send_across(3)
+    first_out[...] = first_full[...].reshape(rank, depth)
 
     pair_copy.wait_recv()
     second_out[...] = adapter_scale_factor * (second_pair[0] + second_pair[1])
 
-    for slot in range(1, 4):
-        across_copy(slot, returned.at[slot], slot, stack(slot)).wait_recv()
     mine = flip(z_high, y) * 2 + flip(z_low, x)
-    out_ref[...] = (
-        (returned[mine].astype(f32) + across[1].astype(f32))
-        + (across[2].astype(f32) + across[3].astype(f32))
-    ).astype(bf16)
+    for part in range(2):
+        rows_here = halves[part]
+        acc[:, rows_here] = jnp.zeros((2, half, rows), f32)
+        for side in range(2):
+            copy = chain_copy(mine, part, side, lax.rem(z + 1, 4))
+
+            @pl.when(z != (0, 3)[side])
+            def _(copy=copy, side=side, rows_here=rows_here):
+                copy.wait_recv()
+                for column in range(2):
+                    place = pl.ds(column * rows, rows)
+                    acc[column, rows_here] += arriving[side, mine, rows_here, place].astype(f32)
+
+        for column in range(2):
+            place = pl.ds(column * rows, rows)
+            out_ref[rows_here, place] = (
+                acc[column, rows_here] + returned[mine, rows_here, place].astype(f32)
+            ).astype(bf16)
 
     for copy in sent:
         copy.wait_send()
-    for copy, to_z in across_sends:
-
-        @pl.when(to_z != z)
+    for copy, active in chain_sends:
+
+        @pl.when(active)
         def _(copy=copy):
             copy.wait_send()
 
@@ -425,9 +464,9 @@
         fused_kernel,
         out_shape=(
             jax.ShapeDtypeStruct((count, depth), bf16),
-            jax.ShapeDtypeStruct((depth, rank), f32),
+            jax.ShapeDtypeStruct((rank, depth), f32),
             jax.ShapeDtypeStruct((rank, width), f32),
-            jax.ShapeDtypeStruct((1, width), f32),
+            jax.ShapeDtypeStruct((width,), f32),
         ),
         in_specs=[away, whole, whole, whole, whole, whole, away, away],
         out_specs=(whole, whole, whole, whole),
@@ -445,30 +484,32 @@
             pltpu.VMEM((2, count, rows), f32),
             pltpu.VMEM((3, count, depth), bf16),
             pltpu.VMEM((4, count, depth), bf16),
-            pltpu.VMEM((4, count, depth), bf16),
+            pltpu.VMEM((2, 4, count, depth), bf16),
             pltpu.VMEM((4, rank, width), f32),
             pltpu.VMEM((2, rank, width), f32),
+            pltpu.VMEM((3, rows, block_scales.shape[1]), bf16),
+            pltpu.VMEM((rows, rank), bf16),
             pltpu.VMEM((8, rank // 8, depth), f32),
             pltpu.VMEM((8, rank // 8, depth), f32),
             pltpu.VMEM((8, rank // 8, depth), f32),
             pltpu.SemaphoreType.DMA((3,)),
-            pltpu.SemaphoreType.DMA((64,)),
-            pltpu.SemaphoreType.DMA((64,)),
+            pltpu.SemaphoreType.DMA((72,)),
+            pltpu.SemaphoreType.DMA((72,)),
         ],
         compiler_params=pltpu.CompilerParams(
             collective_id=0, has_side_effects=True, vmem_limit_bytes=58 * 1024 * 1024
         ),
     )(
         base_codes,
-        block_scales,
-        input_adapter_factor,
+        block_scales.T,
+        input_adapter_factor.T,
         output_adapter_factor,
-        magnitude.reshape(1, width),
+        magnitude,
         inputs,
         grad_out,
         pre_scale,
     )
-    return grad_inputs, first, second, grad_magnitude.reshape(width)
+    return grad_inputs, first.T, second, grad_magnitude
 
 
 def solution(mesh):

time: 138 us -> 121 us (0.88)
  the two profiles are of different devices: /device:TPU:12 before, /device:TPU:6 now
where the time goes in v3:
time: 121 us; the launch traced here: 120 us
  Pallas kernels  115 us (95%)
  local copies, waits for them, and re-layouts  5.05 us (4%)
    pallas_call x1, Pallas kernels, on_device_fused(): pl.pallas_call(fused_kernel, out_shape=(jax.ShapeDtypeStruct((count, dept...  115 us
    unnamed x8, local copies, waits for them, and re-layouts  5.05 us

profile of v3, /device:TPU:6, one launch (start us, length us, event | category | flops | bytes accessed | tf_op | source)
XLA Modules:
  0.0 120.5 jit_solution(13214920905934792736)
XLA Ops:
  0.6 114.8 %shard_map.111 = (bf16[192,1024]{1,0:T(8,128)(2,1)}, f32[64,1024]{1,0:T(8,128)}, f32[64,3584]{1,0:T(8,128)}, f32[3584]{0:T(1024)}) custom-call(s32[512,3584]{1,0:T(8,128)} %codes_hbm.1, f32[56,512]{1,0:T(8,128)} %bitcast.5, bf16[64,4096]{1,0:T(8,128)(2,1)} %bitcast.3, bf16[64,3584]{1,0:T(8,128)(2,1)} %second_ref.1, f32[3584]{0:T(1024)} %magnitude_ref.1, ...), custom_call_target="tpu_custom_call" | custom-call | tf_op jit(solution)/shard_map/pallas_call | solution.py:463
  115.4 0.0 copy-start
  115.4 0.0 copy-start.1
  115.4 1.8 %copy.16 = bf16[192,1024]{1,0:T(8,128)(2,1)} copy(bf16[192,1024]{1,0:T(8,128)(2,1)} %get-tuple-element.16) | data formatting | bytes 786432
  117.3 1.7 %copy.17 = f32[1024,64]{0,1:T(8,128)} copy(f32[1024,64]{0,1:T(8,128)} %bitcast.4) | data formatting | bytes 524288
  118.9 0.0 copy-done
  118.9 0.9 copy.18
  119.9 0.0 copy-done.1
  119.9 0.6 copy.19
Async XLA Ops:
  115.4 3.5 %copy-start = (f32[64,3584]{1,0:T(8,128)S(1)}, f32[64,3584]{1,0:T(8,128)}, u32[]{:S(2)}) copy-start(f32[64,3584]{1,0:T(8,128)} %get-tuple-element.18) | copy-start | bytes 2752516
  115.4 4.5 %copy-start.1 = (f32[3584]{0:T(1024)S(1)}, f32[3584]{0:T(1024)}, u32[]{:S(2)}) copy-start(f32[3584]{0:T(1024)} %get-tuple-element.19) | copy-start | bytes 43012

commit v4 on v2

--- a/solution.py
+++ b/solution.py
@@ -103,10 +103,14 @@
     back_acc,
     acc,
     product,
+    shares,
+    summed,
     returned,
-    across,
+    final,
     second_parts,
     second_pair,
+    pieces,
+    adapter_rows,
     first_split,
     first_recv,
     first_full,
@@ -121,7 +125,7 @@
     tile = COLUMN_TILE
     steps = width // tile
     rank = low.shape[2]
-    block = width // scales_ref.shape[1]
+    block = width // scales_ref.shape[0]
     dp, z = lax.axis_index("dp"), lax.axis_index("tensor")
     core = lax.rem(dp, 2)
     x = lax.rem(dp // 2, 2)
@@ -195,34 +199,40 @@
     from_y.append(remote(grad_hbm.at[lower], tokens.at[2, lower], peer(4)))
 
     depth = inputs_ref.shape[1]
-    low_parts[0] = jnp.dot(
+    nt = (((1,), (1,)), ((), ()))
+    tn = (((0,), (0,)), ((), ()))
+    low_parts[0] = lax.dot_general(
         inputs_ref[...],
-        first_ref[pl.ds(pl.multiple_of(z * depth, depth), depth), :],
+        first_ref[:, pl.ds(pl.multiple_of(z * depth, depth), depth)],
+        nt,
         preferred_element_type=f32,
     ).astype(bf16)
     low_copies = [remote(low_parts.at[0], low_parts.at[r], over(r)) for r in range(1, 4)]
 
     own_rows = pl.ds(pl.multiple_of(dp * rows, rows), rows)
+    adapter_rows[...] = jnp.transpose(first_ref[:, own_rows].astype(f32)).astype(bf16)
+    scales = jnp.transpose(scales_ref[...])
+    high = scales.astype(bf16)
+    rest = scales - high.astype(f32)
+    middle = rest.astype(bf16)
+    pieces[0] = high
+    pieces[1] = middle
+    pieces[2] = (rest - middle.astype(f32)).astype(bf16)
     codes_copy.wait()
     pre_copy.wait()
     own_copy.wait()
 
     def dequantize(step, carry):
         columns = pl.ds(pl.multiple_of(step * tile, tile), tile)
-        scales = scales_ref[...]
-        high = scales.astype(bf16)
-        rest = scales - high.astype(f32)
-        middle = rest.astype(bf16)
-        last = (rest - middle.astype(f32)).astype(bf16)
-        shape = (scales.shape[1], tile)
+        shape = (scales_ref.shape[0], tile)
         place = lax.broadcasted_iota(jnp.int32, shape, 1) // block + step * (tile // block)
         spread = jnp.where(lax.broadcasted_iota(jnp.int32, shape, 0) == place, 1.0, 0.0).astype(bf16)
         expanded = (
-            jnp.dot(high, spread, preferred_element_type=f32)
-            + jnp.dot(middle, spread, preferred_element_type=f32)
-            + jnp.dot(last, spread, preferred_element_type=f32)
+            jnp.dot(pieces[0], spread, preferred_element_type=f32)
+            + jnp.dot(pieces[1], spread, preferred_element_type=f32)
+            + jnp.dot(pieces[2], spread, preferred_element_type=f32)
         )
-        adapter = jnp.dot(first_ref[own_rows, :], second_ref[:, columns], preferred_element_type=f32)
+        adapter = jnp.dot(adapter_rows[...], second_ref[:, columns], preferred_element_type=f32)
         merged = (
             (codes[:, columns].astype(f32) - 7.5) * expanded + adapter_scale_factor * adapter
         ).astype(bf16)
@@ -260,41 +270,65 @@
         (stats[4] + stats[5]) + (stats[6] + stats[7])
     )
     norm = jnp.sqrt(total[0:1, :] + 1e-06)
-    factor[...] = magnitude_ref[...] / norm
-    magnitude_out[...] = total[1:2, :] / norm
+    factor[...] = magnitude_ref[...].reshape(1, width) / norm
+    magnitude_out[...] = (total[1:2, :] / norm).reshape(width)
 
     weight_arrival.wait_recv()
 
-    across_sends = []
-    across_index = used[0]
-    used[0] += 8
-
-    def across_copy(which, source, target_slot, to_z):
+    part = count // 4
+
+    def part_rows(to_z):
+        return pl.ds(pl.multiple_of(to_z * part, part), part)
+
+    def send_shares(which):
+        return [
+            remote(product.at[which, part_rows(stack(r))], shares.at[which, r], over(r))
+            for r in range(1, 4)
+        ]
+
+    def sum_shares(which, copies):
+        for copy in copies:
+            copy.wait_recv()
+        target = returned if which == 0 else summed
+        target[which] = (
+            (product[which, part_rows(z)].astype(f32) + shares[which, 1].astype(f32))
+            + (shares[which, 2].astype(f32) + shares[which, 3].astype(f32))
+        ).astype(bf16)
+        if which == 0:
+            return None
+        return remote(summed.at[which], returned.at[which], peer(2 * which))
+
+    final_sends = []
+    final_index = used[0]
+    used[0] += 4
+
+    def final_copy(which, slot, to_z):
         return pltpu.make_async_remote_copy(
-            src_ref=source,
-            dst_ref=across.at[target_slot],
-            send_sem=send_sem.at[across_index + which],
-            recv_sem=recv_sem.at[across_index + target_slot],
+            src_ref=returned.at[which],
+            dst_ref=final.at[part_rows(z)],
+            send_sem=send_sem.at[final_index + which],
+            recv_sem=recv_sem.at[final_index + slot],
             device_id={"dp": dp, "tensor": to_z},
             device_id_type=MESH,
         )
 
-    def send_across(which):
+    def send_final(which):
         quarter_high, quarter_low = flip(y, which // 2), flip(x, which % 2)
         to_z = quarter_high * 2 + quarter_low
         slot = flip(quarter_high, z_high) * 2 + flip(quarter_low, z_low)
-        copy = across_copy(which, returned.at[which], slot, to_z)
+        copy = final_copy(which, slot, to_z)
 
         @pl.when(to_z != z)
         def _():
             copy.start()
 
-        across_sends.append((copy, to_z))
-
-    nt = (((1,), (1,)), ((), ()))
-    tn = (((0,), (0,)), ((), ()))
-
-    def multiply(which, destination):
+        @pl.when(to_z == z)
+        def _():
+            final[part_rows(z)] = returned[which]
+
+        final_sends.append((copy, to_z))
+
+    def multiply(which):
         acc[...] = jnp.zeros_like(acc)
         if which == 0:
             back_acc[...] = jnp.zeros_like(back_acc)
@@ -317,18 +351,23 @@
 
         lax.fori_loop(0, steps, body, 0)
         for side in range(2):
-            destination[:, pl.ds(side * rows, rows)] = acc[side].astype(bf16)
-
-    multiply(0, returned.at[0])
-    send_across(0)
+            product[which, :, pl.ds(side * rows, rows)] = acc[side].astype(bf16)
+        return send_shares(which)
+
+    shares_0 = multiply(0)
     back_parts[0] = back_acc[...].astype(bf16)
     back_copies = [remote(back_parts.at[0], back_parts.at[r], over(r)) for r in range(1, 4)]
 
-    returns = {}
     from_x[1].wait_recv()
     plane_low[0].wait_recv()
-    multiply(1, product.at[0])
-    returns[1] = remote(product.at[0], returned.at[1], peer(2))
+    shares_1 = multiply(1)
+    sum_shares(0, shares_0)
+    send_final(0)
+
+    from_y[1].wait_recv()
+    plane_low[1].wait_recv()
+    shares_2 = multiply(2)
+    return_1 = sum_shares(1, shares_1)
 
     for copy in back_copies:
         copy.wait_recv()
@@ -343,14 +382,23 @@
     )
     for index in range(slices):
         first_split[index] = gradient[index * piece : (index + 1) * piece, :]
+
+    return_2 = sum_shares(2, shares_2)
+    return_1.wait_recv()
+    send_final(1)
+
+    far_lower.wait_recv()
+    far_upper.wait_recv()
+    plane_low[2].wait_recv()
+    shares_3 = multiply(3)
     first_copies = [
         remote(first_split.at[plane(o)], first_recv.at[o], peer(o)) for o in range(1, 8)
     ]
-
-    from_y[1].wait_recv()
-    plane_low[1].wait_recv()
-    multiply(2, product.at[1])
-    returns[2] = remote(product.at[1], returned.at[2], peer(4))
+    second_pair[0] = (second_parts[0] + second_parts[1]) + (second_parts[2] + second_parts[3])
+    pair_copy = remote(second_pair.at[0], second_pair.at[1], peer(1))
+    return_2.wait_recv()
+    send_final(2)
+    return_3 = sum_shares(3, shares_3)
 
     for copy in first_copies:
         copy.wait_recv()
@@ -362,43 +410,31 @@
     for o in range(1, 8):
         remote(first_full.at[dp], first_full.at[dp], peer(o))
 
-    returns[1].wait_recv()
-    send_across(1)
-    returns[2].wait_recv()
-    send_across(2)
-
-    far_lower.wait_recv()
-    far_upper.wait_recv()
-    plane_low[2].wait_recv()
-    multiply(3, product.at[2])
-    returns[3] = remote(product.at[2], returned.at[3], peer(6))
-
-    second_pair[0] = (second_parts[0] + second_parts[1]) + (second_parts[2] + second_parts[3])
-    pair_copy = remote(second_pair.at[0], second_pair.at[1], peer(1))
-
+    return_3.wait_recv()
+    send_final(3)
+
+    pair_copy.wait_recv()
+    second_out[...] = adapter_scale_factor * (second_pair[0] + second_pair[1])
     for o in range(1, 8):
         arrival(
             first_full.at[dp], first_full.at[plane(o)], first_index + o - 1, peer(o)
         ).wait_recv()
-    first_out[...] = jnp.transpose(first_full[...].reshape(rank, depth))
-
-    returns[3].wait_recv()
-    send_across(3)
-
-    pair_copy.wait_recv()
-    second_out[...] = adapter_scale_factor * (second_pair[0] + second_pair[1])
+    first_out[...] = first_full[...].reshape(rank, depth)
 
     for slot in range(1, 4):
-        across_copy(slot, returned.at[slot], slot, stack(slot)).wait_recv()
-    mine = flip(z_high, y) * 2 + flip(z_low, x)
-    out_ref[...] = (
-        (returned[mine].astype(f32) + across[1].astype(f32))
-        + (across[2].astype(f32) + across[3].astype(f32))
-    ).astype(bf16)
+        pltpu.make_async_remote_copy(
+            src_ref=returned.at[slot],
+            dst_ref=final.at[part_rows(stack(slot))],
+            send_sem=send_sem.at[final_index + slot],
+            recv_sem=recv_sem.at[final_index + slot],
+            device_id=over(slot),
+            device_id_type=MESH,
+        ).wait_recv()
+    out_ref[...] = final[...]
 
     for copy in sent:
         copy.wait_send()
-    for copy, to_z in across_sends:
+    for copy, to_z in final_sends:
 
         @pl.when(to_z != z)
         def _(copy=copy):
@@ -425,9 +461,9 @@
         fused_kernel,
         out_shape=(
             jax.ShapeDtypeStruct((count, depth), bf16),
-            jax.ShapeDtypeStruct((depth, rank), f32),
+            jax.ShapeDtypeStruct((rank, depth), f32),
             jax.ShapeDtypeStruct((rank, width), f32),
-            jax.ShapeDtypeStruct((1, width), f32),
+            jax.ShapeDtypeStruct((width,), f32),
         ),
         in_specs=[away, whole, whole, whole, whole, whole, away, away],
         out_specs=(whole, whole, whole, whole),
@@ -443,32 +479,36 @@
             pltpu.VMEM((4, count, rank), bf16),
             pltpu.VMEM((count, rank), f32),
             pltpu.VMEM((2, count, rows), f32),
-            pltpu.VMEM((3, count, depth), bf16),
             pltpu.VMEM((4, count, depth), bf16),
-            pltpu.VMEM((4, count, depth), bf16),
+            pltpu.VMEM((4, 4, count // 4, depth), bf16),
+            pltpu.VMEM((4, count // 4, depth), bf16),
+            pltpu.VMEM((4, count // 4, depth), bf16),
+            pltpu.VMEM((count, depth), bf16),
             pltpu.VMEM((4, rank, width), f32),
             pltpu.VMEM((2, rank, width), f32),
+            pltpu.VMEM((3, rows, block_scales.shape[1]), bf16),
+            pltpu.VMEM((rows, rank), bf16),
             pltpu.VMEM((8, rank // 8, depth), f32),
             pltpu.VMEM((8, rank // 8, depth), f32),
             pltpu.VMEM((8, rank // 8, depth), f32),
             pltpu.SemaphoreType.DMA((3,)),
-            pltpu.SemaphoreType.DMA((64,)),
-            pltpu.SemaphoreType.DMA((64,)),
+            pltpu.SemaphoreType.DMA((72,)),
+            pltpu.SemaphoreType.DMA((72,)),
         ],
         compiler_params=pltpu.CompilerParams(
             collective_id=0, has_side_effects=True, vmem_limit_bytes=58 * 1024 * 1024
         ),
     )(
         base_codes,
-        block_scales,
-        input_adapter_factor,
+        block_scales.T,
+        input_adapter_factor.T,
         output_adapter_factor,
-        magnitude.reshape(1, width),
+        magnitude,
         inputs,
         grad_out,
         pre_scale,
     )
-    return grad_inputs, first, second, grad_magnitude.reshape(width)
+    return grad_inputs, first.T, second, grad_magnitude
 
 
 def solution(mesh):

time: 138 us -> 116 us (0.84)
  Pallas kernels: 125 us -> 109 us
  local copies, waits for them, and re-layouts: 10.1 us -> 5.05 us
  other arithmetic: 1.44 us -> 0 us
    pallas_call x1, Pallas kernels: 125 us -> 109 us  [on_device_fused(): pl.pallas_call(fused_kernel, out_shape=(jax.ShapeDtypeStruct((count, dept...]
    unnamed x7 -> x8, local copies, waits for them, and re-layouts: 8.73 us -> 5.05 us
    pallas_call x1 -> x0, other arithmetic: 1.44 us -> none  [on_device_fused(): pl.pallas_call(fused_kernel, out_shape=(jax.ShapeDtypeStruct((count, dept...]
where the time goes in v4:
time: 116 us; the launch traced here: 115 us
  Pallas kernels  109 us (94%)
  local copies, waits for them, and re-layouts  5.05 us (4%)
    pallas_call x1, Pallas kernels, on_device_fused(): pl.pallas_call(fused_kernel, out_shape=(jax.ShapeDtypeStruct((count, dept...  109 us
    unnamed x8, local copies, waits for them, and re-layouts  5.05 us

profile of v4, /device:TPU:12, one launch (start us, length us, event | category | flops | bytes accessed | tf_op | source)
XLA Modules:
  0.0 114.9 jit_solution(15614903161857400369)
XLA Ops:
  0.6 109.2 %shard_map.111 = (bf16[192,1024]{1,0:T(8,128)(2,1)}, f32[64,1024]{1,0:T(8,128)}, f32[64,3584]{1,0:T(8,128)}, f32[3584]{0:T(1024)}) custom-call(s32[512,3584]{1,0:T(8,128)} %codes_hbm.1, f32[56,512]{1,0:T(8,128)} %bitcast.5, bf16[64,4096]{1,0:T(8,128)(2,1)} %bitcast.3, bf16[64,3584]{1,0:T(8,128)(2,1)} %second_ref.1, f32[3584]{0:T(1024)} %magnitude_ref.1, ...), custom_call_target="tpu_custom_call" | custom-call | tf_op jit(solution)/shard_map/pallas_call | solution.py:460
  109.8 0.0 copy-start
  109.9 0.0 copy-start.1
  109.9 1.8 %copy.16 = bf16[192,1024]{1,0:T(8,128)(2,1)} copy(bf16[192,1024]{1,0:T(8,128)(2,1)} %get-tuple-element.16) | data formatting | bytes 786432
  111.7 1.7 %copy.17 = f32[1024,64]{0,1:T(8,128)} copy(f32[1024,64]{0,1:T(8,128)} %bitcast.4) | data formatting | bytes 524288
  113.4 0.0 copy-done
  113.4 0.9 copy.18
  114.3 0.0 copy-done.1
  114.3 0.6 copy.19
Async XLA Ops:
  109.8 3.5 %copy-start = (f32[64,3584]{1,0:T(8,128)S(1)}, f32[64,3584]{1,0:T(8,128)}, u32[]{:S(2)}) copy-start(f32[64,3584]{1,0:T(8,128)} %get-tuple-element.18) | copy-start | bytes 2752516
  109.9 4.5 %copy-start.1 = (f32[3584]{0:T(1024)S(1)}, f32[3584]{0:T(1024)}, u32[]{:S(2)}) copy-start(f32[3584]{0:T(1024)} %get-tuple-element.19) | copy-start | bytes 43012

commit v5 on v4

--- a/solution.py
+++ b/solution.py
@@ -101,7 +101,7 @@
     low,
     back_parts,
     back_acc,
-    acc,
+    scaled,
     product,
     shares,
     summed,
@@ -122,6 +122,7 @@
     rows, width = codes.shape
     count = tokens.shape[1]
     half = count // 2
+    group = rows // 2
     tile = COLUMN_TILE
     steps = width // tile
     rank = low.shape[2]
@@ -211,13 +212,11 @@
 
     own_rows = pl.ds(pl.multiple_of(dp * rows, rows), rows)
     adapter_rows[...] = jnp.transpose(first_ref[:, own_rows].astype(f32)).astype(bf16)
-    scales = jnp.transpose(scales_ref[...])
-    high = scales.astype(bf16)
-    rest = scales - high.astype(f32)
-    middle = rest.astype(bf16)
-    pieces[0] = high
-    pieces[1] = middle
-    pieces[2] = (rest - middle.astype(f32)).astype(bf16)
+    scales = scales_ref[...]
+    high = scales.astype(bf16).astype(f32)
+    middle = (scales - high).astype(bf16).astype(f32)
+    last = (scales - high) - middle
+    pieces[...] = jnp.transpose(jnp.concatenate([high, middle, last], axis=0)).astype(bf16)
     codes_copy.wait()
     pre_copy.wait()
     own_copy.wait()
@@ -226,17 +225,15 @@
         columns = pl.ds(pl.multiple_of(step * tile, tile), tile)
         shape = (scales_ref.shape[0], tile)
         place = lax.broadcasted_iota(jnp.int32, shape, 1) // block + step * (tile // block)
-        spread = jnp.where(lax.broadcasted_iota(jnp.int32, shape, 0) == place, 1.0, 0.0).astype(bf16)
-        expanded = (
-            jnp.dot(pieces[0], spread, preferred_element_type=f32)
-            + jnp.dot(pieces[1], spread, preferred_element_type=f32)
-            + jnp.dot(pieces[2], spread, preferred_element_type=f32)
-        )
+        chosen = jnp.where(lax.broadcasted_iota(jnp.int32, shape, 0) == place, 1.0, 0.0)
+        spread = jnp.concatenate([chosen, chosen, chosen], axis=0).astype(bf16)
+        expanded = jnp.dot(pieces[...], spread, preferred_element_type=f32)
         adapter = jnp.dot(adapter_rows[...], second_ref[:, columns], preferred_element_type=f32)
         merged = (
             (codes[:, columns].astype(f32) - 7.5) * expanded + adapter_scale_factor * adapter
         ).astype(bf16)
-        weight[core, :, columns] = merged
+        weight[core * 2, :, columns] = merged[:group]
+        weight[core * 2 + 1, :, columns] = merged[group:]
         merged_f = merged.astype(f32)
         stats[0, 0:1, columns] = jnp.sum(merged_f * merged_f, axis=0, keepdims=True)
         stats[0, 1:2, columns] = jnp.sum(
@@ -248,8 +245,11 @@
 
     stats_copies = [remote(stats.at[0], stats.at[o], peer(o)) for o in range(1, 8)]
     weight_index = used[0]
-    remote(weight.at[core], weight.at[core], peer(1))
-    weight_arrival = arrival(weight.at[core], weight.at[1 - core], weight_index, peer(1))
+    own_half, other_half = pl.ds(core * 2, 2), pl.ds(2 - core * 2, 2)
+    remote(weight.at[own_half], weight.at[own_half], peer(1))
+    weight_arrival = arrival(
+        weight.at[own_half], weight.at[other_half], weight_index, peer(1)
+    )
 
     for copy in low_copies:
         copy.wait_recv()
@@ -280,79 +280,103 @@
     def part_rows(to_z):
         return pl.ds(pl.multiple_of(to_z * part, part), part)
 
-    def send_shares(which):
+    full = pl.ds(0, depth)
+    groups = [pl.ds(n * group, group) for n in range(4)]
+
+    def send_shares(which, columns):
         return [
-            remote(product.at[which, part_rows(stack(r))], shares.at[which, r], over(r))
+            remote(
+                product.at[which, part_rows(stack(r)), columns],
+                shares.at[which, r, :, columns],
+                over(r),
+            )
             for r in range(1, 4)
         ]
 
-    def sum_shares(which, copies):
+    def sum_shares(which, copies, columns):
         for copy in copies:
             copy.wait_recv()
         target = returned if which == 0 else summed
-        target[which] = (
-            (product[which, part_rows(z)].astype(f32) + shares[which, 1].astype(f32))
-            + (shares[which, 2].astype(f32) + shares[which, 3].astype(f32))
+        target[which, :, columns] = (
+            (product[which, part_rows(z), columns].astype(f32) + shares[which, 1, :, columns].astype(f32))
+            + (shares[which, 2, :, columns].astype(f32) + shares[which, 3, :, columns].astype(f32))
         ).astype(bf16)
         if which == 0:
             return None
-        return remote(summed.at[which], returned.at[which], peer(2 * which))
+        return remote(
+            summed.at[which, :, columns], returned.at[which, :, columns], peer(2 * which)
+        )
 
     final_sends = []
     final_index = used[0]
-    used[0] += 4
-
-    def final_copy(which, slot, to_z):
+    used[0] += 16
+
+    def final_copy(which, slot, n, target_rows, to):
         return pltpu.make_async_remote_copy(
-            src_ref=returned.at[which],
-            dst_ref=final.at[part_rows(z)],
-            send_sem=send_sem.at[final_index + which],
-            recv_sem=recv_sem.at[final_index + slot],
-            device_id={"dp": dp, "tensor": to_z},
+            src_ref=returned.at[which, :, groups[n]],
+            dst_ref=final.at[target_rows, groups[n]],
+            send_sem=send_sem.at[final_index + which * 4 + n],
+            recv_sem=recv_sem.at[final_index + slot * 4 + n],
+            device_id=to,
             device_id_type=MESH,
         )
 
-    def send_final(which):
+    def send_final(which, pieces_sent=range(4)):
         quarter_high, quarter_low = flip(y, which // 2), flip(x, which % 2)
         to_z = quarter_high * 2 + quarter_low
         slot = flip(quarter_high, z_high) * 2 + flip(quarter_low, z_low)
-        copy = final_copy(which, slot, to_z)
-
-        @pl.when(to_z != z)
-        def _():
-            copy.start()
-
-        @pl.when(to_z == z)
-        def _():
-            final[part_rows(z)] = returned[which]
-
-        final_sends.append((copy, to_z))
-
-    def multiply(which):
-        acc[...] = jnp.zeros_like(acc)
+        for n in pieces_sent:
+            copy = final_copy(which, slot, n, part_rows(z), {"dp": dp, "tensor": to_z})
+
+            @pl.when(to_z != z)
+            def _(copy=copy):
+                copy.start()
+
+            @pl.when(to_z == z)
+            def _(n=n):
+                final[part_rows(z), groups[n]] = returned[which, :, groups[n]]
+
+            final_sends.append((copy, to_z))
+
+    def scale_tokens(which):
+        def body(step, carry):
+            columns = pl.ds(pl.multiple_of(step * tile, tile), tile)
+            scaled[:, columns] = (
+                tokens[which, :, columns].astype(f32) * factor[:, columns]
+            ).astype(bf16)
+            return carry
+
+        lax.fori_loop(0, steps, body, 0)
+
+    def multiply_group(which, n):
+        product[which, :, groups[n]] = lax.dot_general(
+            scaled[...], weight[n], nt, preferred_element_type=f32
+        ).astype(bf16)
+
+    def second_product(which):
         if which == 0:
             back_acc[...] = jnp.zeros_like(back_acc)
 
         def body(step, carry):
             columns = pl.ds(pl.multiple_of(step * tile, tile), tile)
-            scaled = (tokens[which, :, columns].astype(f32) * factor[:, columns]).astype(bf16)
-            for side in range(2):
-                acc[side] += lax.dot_general(
-                    scaled, weight[side, :, columns], nt, preferred_element_type=f32
-                )
             second_parts[which, :, columns] = lax.dot_general(
-                low[which], scaled, tn, preferred_element_type=f32
+                low[which], scaled[:, columns], tn, preferred_element_type=f32
             )
             if which == 0:
                 back_acc[...] += lax.dot_general(
-                    scaled, second_ref[:, columns], nt, preferred_element_type=f32
+                    scaled[:, columns], second_ref[:, columns], nt, preferred_element_type=f32
                 )
             return carry
 
         lax.fori_loop(0, steps, body, 0)
-        for side in range(2):
-            product[which, :, pl.ds(side * rows, rows)] = acc[side].astype(bf16)
-        return send_shares(which)
+
+    def multiply(which):
+        scale_tokens(which)
+        for n in range(4):
+            multiply_group(which, n)
+        copies = send_shares(which, full)
+        second_product(which)
+        return copies
 
     shares_0 = multiply(0)
     back_parts[0] = back_acc[...].astype(bf16)
@@ -361,13 +385,13 @@
     from_x[1].wait_recv()
     plane_low[0].wait_recv()
     shares_1 = multiply(1)
-    sum_shares(0, shares_0)
+    sum_shares(0, shares_0, full)
     send_final(0)
 
     from_y[1].wait_recv()
     plane_low[1].wait_recv()
     shares_2 = multiply(2)
-    return_1 = sum_shares(1, shares_1)
+    return_1 = sum_shares(1, shares_1, full)
 
     for copy in back_copies:
         copy.wait_recv()
@@ -383,22 +407,31 @@
     for index in range(slices):
         first_split[index] = gradient[index * piece : (index + 1) * piece, :]
 
-    return_2 = sum_shares(2, shares_2)
+    return_2 = sum_shares(2, shares_2, full)
     return_1.wait_recv()
     send_final(1)
 
     far_lower.wait_recv()
     far_upper.wait_recv()
     plane_low[2].wait_recv()
-    shares_3 = multiply(3)
+    scale_tokens(3)
+    shares_3 = []
+    for n in range(4):
+        multiply_group(3, n)
+        shares_3.append(send_shares(3, groups[n]))
+    return_2.wait_recv()
+    send_final(2)
+    returns_3 = [sum_shares(3, shares_3[n], groups[n]) for n in range(2)]
+    second_product(3)
+    returns_3 += [sum_shares(3, shares_3[n], groups[n]) for n in range(2, 4)]
     first_copies = [
         remote(first_split.at[plane(o)], first_recv.at[o], peer(o)) for o in range(1, 8)
     ]
     second_pair[0] = (second_parts[0] + second_parts[1]) + (second_parts[2] + second_parts[3])
     pair_copy = remote(second_pair.at[0], second_pair.at[1], peer(1))
-    return_2.wait_recv()
-    send_final(2)
-    return_3 = sum_shares(3, shares_3)
+    for n in range(4):
+        returns_3[n].wait_recv()
+        send_final(3, (n,))
 
     for copy in first_copies:
         copy.wait_recv()
@@ -410,9 +443,6 @@
     for o in range(1, 8):
         remote(first_full.at[dp], first_full.at[dp], peer(o))
 
-    return_3.wait_recv()
-    send_final(3)
-
     pair_copy.wait_recv()
     second_out[...] = adapter_scale_factor * (second_pair[0] + second_pair[1])
     for o in range(1, 8):
@@ -421,15 +451,9 @@
         ).wait_recv()
     first_out[...] = first_full[...].reshape(rank, depth)
 
-    for slot in range(1, 4):
-        pltpu.make_async_remote_copy(
-            src_ref=returned.at[slot],
-            dst_ref=final.at[part_rows(stack(slot))],
-            send_sem=send_sem.at[final_index + slot],
-            recv_sem=recv_sem.at[final_index + slot],
-            device_id=over(slot),
-            device_id_type=MESH,
-        ).wait_recv()
+    for n in range(4):
+        for slot in range(1, 4):
+            final_copy(slot, slot, n, part_rows(stack(slot)), over(slot)).wait_recv()
     out_ref[...] = final[...]
 
     for copy in sent:
@@ -471,14 +495,14 @@
             pltpu.VMEM((rows, width), jnp.int32),
             pltpu.VMEM((count, width), bf16),
             pltpu.VMEM((4, count, width), bf16),
-            pltpu.VMEM((2, rows, width), bf16),
+            pltpu.VMEM((4, rows // 2, width), bf16),
             pltpu.VMEM((8, 2, width), f32),
             pltpu.VMEM((1, width), f32),
             pltpu.VMEM((4, count, rank), bf16),
             pltpu.VMEM((4, count, rank), bf16),
             pltpu.VMEM((4, count, rank), bf16),
             pltpu.VMEM((count, rank), f32),
-            pltpu.VMEM((2, count, rows), f32),
+            pltpu.VMEM((count, width), bf16),
             pltpu.VMEM((4, count, depth), bf16),
             pltpu.VMEM((4, 4, count // 4, depth), bf16),
             pltpu.VMEM((4, count // 4, depth), bf16),
@@ -486,14 +510,14 @@
             pltpu.VMEM((count, depth), bf16),
             pltpu.VMEM((4, rank, width), f32),
             pltpu.VMEM((2, rank, width), f32),
-            pltpu.VMEM((3, rows, block_scales.shape[1]), bf16),
+            pltpu.VMEM((rows, 3 * block_scales.shape[1]), bf16),
             pltpu.VMEM((rows, rank), bf16),
             pltpu.VMEM((8, rank // 8, depth), f32),
             pltpu.VMEM((8, rank // 8, depth), f32),
             pltpu.VMEM((8, rank // 8, depth), f32),
             pltpu.SemaphoreType.DMA((3,)),
-            pltpu.SemaphoreType.DMA((72,)),
-            pltpu.SemaphoreType.DMA((72,)),
+            pltpu.SemaphoreType.DMA((96,)),
+            pltpu.SemaphoreType.DMA((96,)),
         ],
         compiler_params=pltpu.CompilerParams(
             collective_id=0, has_side_effects=True, vmem_limit_bytes=58 * 1024 * 1024

time: 116 us -> 117 us (level)
  no operation moved by 1% of the time
where the time goes in v5:
time: 117 us; the launch traced here: 115 us
  Pallas kernels  109 us (93%)
  local copies, waits for them, and re-layouts  5.05 us (4%)
    pallas_call x1, Pallas kernels, on_device_fused(): pl.pallas_call(fused_kernel, out_shape=(jax.ShapeDtypeStruct((count, dept...  109 us
    unnamed x8, local copies, waits for them, and re-layouts  5.05 us

profile of v5, /device:TPU:12, one launch (start us, length us, event | category | flops | bytes accessed | tf_op | source)
XLA Modules:
  0.0 114.9 jit_solution(12716671399278087190)
XLA Ops:
  0.6 109.2 %shard_map.111 = (bf16[192,1024]{1,0:T(8,128)(2,1)}, f32[64,1024]{1,0:T(8,128)}, f32[64,3584]{1,0:T(8,128)}, f32[3584]{0:T(1024)}) custom-call(s32[512,3584]{1,0:T(8,128)} %codes_hbm.1, f32[56,512]{1,0:T(8,128)} %bitcast.5, bf16[64,4096]{1,0:T(8,128)(2,1)} %bitcast.3, bf16[64,3584]{1,0:T(8,128)(2,1)} %second_ref.1, f32[3584]{0:T(1024)} %magnitude_ref.1, ...), custom_call_target="tpu_custom_call" | custom-call | tf_op jit(solution)/shard_map/pallas_call | solution.py:484
  109.9 0.0 copy-start
  109.9 0.0 copy-start.1
  109.9 1.8 %copy.16 = bf16[192,1024]{1,0:T(8,128)(2,1)} copy(bf16[192,1024]{1,0:T(8,128)(2,1)} %get-tuple-element.16) | data formatting | bytes 786432
  111.7 1.7 %copy.17 = f32[1024,64]{0,1:T(8,128)} copy(f32[1024,64]{0,1:T(8,128)} %bitcast.4) | data formatting | bytes 524288
  113.4 0.0 copy-done
  113.4 0.9 copy.18
  114.3 0.0 copy-done.1
  114.3 0.6 copy.19
Async XLA Ops:
  109.9 3.5 %copy-start = (f32[64,3584]{1,0:T(8,128)S(1)}, f32[64,3584]{1,0:T(8,128)}, u32[]{:S(2)}) copy-start(f32[64,3584]{1,0:T(8,128)} %get-tuple-element.18) | copy-start | bytes 2752516
  109.9 4.5 %copy-start.1 = (f32[3584]{0:T(1024)S(1)}, f32[3584]{0:T(1024)}, u32[]{:S(2)}) copy-start(f32[3584]{0:T(1024)} %get-tuple-element.19) | copy-start | bytes 43012

commit v6 on v5

--- a/solution.py
+++ b/solution.py
@@ -196,8 +196,6 @@
     from_y = [
         remote(grad_hbm.at[upper], tokens.at[2, upper], peer(4)),
     ]
-    from_x.append(remote(grad_hbm.at[upper], tokens.at[1, upper], peer(2)))
-    from_y.append(remote(grad_hbm.at[lower], tokens.at[2, lower], peer(4)))
 
     depth = inputs_ref.shape[1]
     nt = (((1,), (1,)), ((), ()))
@@ -250,6 +248,8 @@
     weight_arrival = arrival(
         weight.at[own_half], weight.at[other_half], weight_index, peer(1)
     )
+    from_x.append(remote(grad_hbm.at[upper], tokens.at[1, upper], peer(2)))
+    from_y.append(remote(grad_hbm.at[lower], tokens.at[2, lower], peer(4)))
 
     for copy in low_copies:
         copy.wait_recv()
@@ -259,11 +259,6 @@
     ).astype(bf16)
     plane_low = [remote(low.at[0], low.at[b], peer(2 * b)) for b in range(1, 4)]
 
-    from_x[0].wait_recv()
-    far_lower = remote(tokens.at[1, lower], tokens.at[3, lower], peer(4))
-    from_y[0].wait_recv()
-    far_upper = remote(tokens.at[2, upper], tokens.at[3, upper], peer(2))
-
     for copy in stats_copies:
         copy.wait_recv()
     total = ((stats[0] + stats[1]) + (stats[2] + stats[3])) + (
@@ -272,8 +267,6 @@
     norm = jnp.sqrt(total[0:1, :] + 1e-06)
     factor[...] = magnitude_ref[...].reshape(1, width) / norm
     magnitude_out[...] = (total[1:2, :] / norm).reshape(width)
-
-    weight_arrival.wait_recv()
 
     part = count // 4
 
@@ -297,6 +290,11 @@
         for copy in copies:
             copy.wait_recv()
         target = returned if which == 0 else summed
+        slot, to = which, peer(2 * which)
+        if which in (1, 2):
+            slot = 1 + z_high if which == 1 else 2 - z_high
+            to_y, to_x = flip(y, slot - 1), flip(x, 2 - slot)
+            to = {"dp": to_y * 4 + to_x * 2 + core, "tensor": z}
         target[which, :, columns] = (
             (product[which, part_rows(z), columns].astype(f32) + shares[which, 1, :, columns].astype(f32))
             + (shares[which, 2, :, columns].astype(f32) + shares[which, 3, :, columns].astype(f32))
@@ -304,29 +302,33 @@
         if which == 0:
             return None
         return remote(
-            summed.at[which, :, columns], returned.at[which, :, columns], peer(2 * which)
+            summed.at[which, :, columns], returned.at[slot, :, columns], to
         )
 
     final_sends = []
     final_index = used[0]
     used[0] += 16
 
-    def final_copy(which, slot, n, target_rows, to):
+    def final_copy(which, tag, slot, n, target_rows, to):
         return pltpu.make_async_remote_copy(
             src_ref=returned.at[which, :, groups[n]],
             dst_ref=final.at[target_rows, groups[n]],
-            send_sem=send_sem.at[final_index + which * 4 + n],
+            send_sem=send_sem.at[final_index + tag * 4 + n],
             recv_sem=recv_sem.at[final_index + slot * 4 + n],
             device_id=to,
             device_id_type=MESH,
         )
 
-    def send_final(which, pieces_sent=range(4)):
-        quarter_high, quarter_low = flip(y, which // 2), flip(x, which % 2)
+    def send_final(tag, pieces_sent=range(4)):
+        which, over_y, over_x = tag, tag // 2, tag % 2
+        if tag in (1, 2):
+            which = 1 + z_high if tag == 1 else 2 - z_high
+            over_y, over_x = which - 1, 2 - which
+        quarter_high, quarter_low = flip(y, over_y), flip(x, over_x)
         to_z = quarter_high * 2 + quarter_low
         slot = flip(quarter_high, z_high) * 2 + flip(quarter_low, z_low)
         for n in pieces_sent:
-            copy = final_copy(which, slot, n, part_rows(z), {"dp": dp, "tensor": to_z})
+            copy = final_copy(which, tag, slot, n, part_rows(z), {"dp": dp, "tensor": to_z})
 
             @pl.when(to_z != z)
             def _(copy=copy):
@@ -338,18 +340,20 @@
 
             final_sends.append((copy, to_z))
 
-    def scale_tokens(which):
+    def scale_tokens(lower_block, upper_block):
         def body(step, carry):
             columns = pl.ds(pl.multiple_of(step * tile, tile), tile)
-            scaled[:, columns] = (
-                tokens[which, :, columns].astype(f32) * factor[:, columns]
-            ).astype(bf16)
+            for which, part in ((lower_block, lower), (upper_block, upper)):
+                scaled[part, columns] = (
+                    tokens[which, part, columns].astype(f32) * factor[:, columns]
+                ).astype(bf16)
             return carry
 
         lax.fori_loop(0, steps, body, 0)
 
     def multiply_group(which, n):
-        product[which, :, groups[n]] = lax.dot_general(
+        columns = pl.ds(pl.multiple_of(n * group, group), group)
+        product[which, :, columns] = lax.dot_general(
             scaled[...], weight[n], nt, preferred_element_type=f32
         ).astype(bf16)
 
@@ -359,39 +363,54 @@
 
         def body(step, carry):
             columns = pl.ds(pl.multiple_of(step * tile, tile), tile)
+            values = (tokens[which, :, columns].astype(f32) * factor[:, columns]).astype(bf16)
             second_parts[which, :, columns] = lax.dot_general(
-                low[which], scaled[:, columns], tn, preferred_element_type=f32
+                low[which], values, tn, preferred_element_type=f32
             )
             if which == 0:
                 back_acc[...] += lax.dot_general(
-                    scaled[:, columns], second_ref[:, columns], nt, preferred_element_type=f32
+                    values, second_ref[:, columns], nt, preferred_element_type=f32
                 )
             return carry
 
         lax.fori_loop(0, steps, body, 0)
 
-    def multiply(which):
-        scale_tokens(which)
-        for n in range(4):
-            multiply_group(which, n)
-        copies = send_shares(which, full)
-        second_product(which)
-        return copies
-
-    shares_0 = multiply(0)
+    scale_tokens(0, 0)
+    for n in range(2):
+        multiply_group(0, core * 2 + n)
+    weight_arrival.wait_recv()
+    for n in range(2):
+        multiply_group(0, 2 - core * 2 + n)
+    shares_0 = send_shares(0, full)
+
+    from_x[0].wait_recv()
+    far_lower = remote(tokens.at[1, lower], tokens.at[3, lower], peer(4))
+    from_y[0].wait_recv()
+    far_upper = remote(tokens.at[2, upper], tokens.at[3, upper], peer(2))
+
+    scale_tokens(1, 2)
+    for n in range(4):
+        multiply_group(1, n)
+    shares_1 = send_shares(1, full)
+
+    second_product(0)
     back_parts[0] = back_acc[...].astype(bf16)
     back_copies = [remote(back_parts.at[0], back_parts.at[r], over(r)) for r in range(1, 4)]
-
-    from_x[1].wait_recv()
-    plane_low[0].wait_recv()
-    shares_1 = multiply(1)
     sum_shares(0, shares_0, full)
     send_final(0)
 
+    from_x[1].wait_recv()
     from_y[1].wait_recv()
+    scale_tokens(2, 1)
+    for n in range(4):
+        multiply_group(2, n)
+    shares_2 = send_shares(2, full)
+    return_1 = sum_shares(1, shares_1, full)
+
+    plane_low[0].wait_recv()
+    second_product(1)
     plane_low[1].wait_recv()
-    shares_2 = multiply(2)
-    return_1 = sum_shares(1, shares_1, full)
+    second_product(2)
 
     for copy in back_copies:
         copy.wait_recv()
@@ -407,14 +426,14 @@
     for index in range(slices):
         first_split[index] = gradient[index * piece : (index + 1) * piece, :]
 
-    return_2 = sum_shares(2, shares_2, full)
     return_1.wait_recv()
     send_final(1)
+    return_2 = sum_shares(2, shares_2, full)
 
     far_lower.wait_recv()
     far_upper.wait_recv()
     plane_low[2].wait_recv()
-    scale_tokens(3)
+    scale_tokens(3, 3)
     shares_3 = []
     for n in range(4):
         multiply_group(3, n)
@@ -453,7 +472,7 @@
 
     for n in range(4):
         for slot in range(1, 4):
-            final_copy(slot, slot, n, part_rows(stack(slot)), over(slot)).wait_recv()
+            final_copy(slot, slot, slot, n, part_rows(stack(slot)), over(slot)).wait_recv()
     out_ref[...] = final[...]
 
     for copy in sent:

time: 117 us -> 100 us (0.85)
  Pallas kernels: 109 us -> 92.4 us
    pallas_call x1, Pallas kernels: 109 us -> 92.4 us  [on_device_fused(): pl.pallas_call(fused_kernel, out_shape=(jax.ShapeDtypeStruct((count, dept...]
where the time goes in v6:
time: 100 us; the launch traced here: 98.1 us
  Pallas kernels  92.4 us (92%)
  local copies, waits for them, and re-layouts  5.05 us (5%)
    pallas_call x1, Pallas kernels, on_device_fused(): pl.pallas_call(fused_kernel, out_shape=(jax.ShapeDtypeStruct((count, dept...  92.4 us
    unnamed x8, local copies, waits for them, and re-layouts  5.05 us

profile of v6, /device:TPU:12, one launch (start us, length us, event | category | flops | bytes accessed | tf_op | source)
XLA Modules:
  0.0 98.1 jit_solution(14967578099071961517)
XLA Ops:
  0.6 92.4 %shard_map.111 = (bf16[192,1024]{1,0:T(8,128)(2,1)}, f32[64,1024]{1,0:T(8,128)}, f32[64,3584]{1,0:T(8,128)}, f32[3584]{0:T(1024)}) custom-call(s32[512,3584]{1,0:T(8,128)} %codes_hbm.1, f32[56,512]{1,0:T(8,128)} %bitcast.5, bf16[64,4096]{1,0:T(8,128)(2,1)} %bitcast.3, bf16[64,3584]{1,0:T(8,128)(2,1)} %second_ref.1, f32[3584]{0:T(1024)} %magnitude_ref.1, ...), custom_call_target="tpu_custom_call" | custom-call | tf_op jit(solution)/shard_map/pallas_call | solution.py:503
  93.0 0.0 copy-start
  93.0 0.0 copy-start.1
  93.0 1.8 %copy.16 = bf16[192,1024]{1,0:T(8,128)(2,1)} copy(bf16[192,1024]{1,0:T(8,128)(2,1)} %get-tuple-element.16) | data formatting | bytes 786432
  94.9 1.7 %copy.17 = f32[1024,64]{0,1:T(8,128)} copy(f32[1024,64]{0,1:T(8,128)} %bitcast.4) | data formatting | bytes 524288
  96.5 0.0 copy-done
  96.5 0.9 copy.18
  97.5 0.0 copy-done.1
  97.5 0.6 copy.19
Async XLA Ops:
  93.0 3.5 %copy-start = (f32[64,3584]{1,0:T(8,128)S(1)}, f32[64,3584]{1,0:T(8,128)}, u32[]{:S(2)}) copy-start(f32[64,3584]{1,0:T(8,128)} %get-tuple-element.18) | copy-start | bytes 2752516
  93.0 4.5 %copy-start.1 = (f32[3584]{0:T(1024)S(1)}, f32[3584]{0:T(1024)}, u32[]{:S(2)}) copy-start(f32[3584]{0:T(1024)} %get-tuple-element.19) | copy-start | bytes 43012

commit v7 on v6

--- a/solution.py
+++ b/solution.py
@@ -239,7 +239,10 @@
         )
         return carry
 
-    lax.fori_loop(0, steps, dequantize, 0)
+    lax.fori_loop(0, steps // 2, dequantize, 0)
+    from_x.append(remote(grad_hbm.at[upper], tokens.at[1, upper], peer(2)))
+    from_y.append(remote(grad_hbm.at[lower], tokens.at[2, lower], peer(4)))
+    lax.fori_loop(steps // 2, steps, dequantize, 0)
 
     stats_copies = [remote(stats.at[0], stats.at[o], peer(o)) for o in range(1, 8)]
     weight_index = used[0]
@@ -248,8 +251,6 @@
     weight_arrival = arrival(
         weight.at[own_half], weight.at[other_half], weight_index, peer(1)
     )
-    from_x.append(remote(grad_hbm.at[upper], tokens.at[1, upper], peer(2)))
-    from_y.append(remote(grad_hbm.at[lower], tokens.at[2, lower], peer(4)))
 
     for copy in low_copies:
         copy.wait_recv()
@@ -378,15 +379,15 @@
     scale_tokens(0, 0)
     for n in range(2):
         multiply_group(0, core * 2 + n)
+    from_x[0].wait_recv()
+    far_lower = remote(tokens.at[1, lower], tokens.at[3, lower], peer(4))
+    from_y[0].wait_recv()
+    far_upper = remote(tokens.at[2, upper], tokens.at[3, upper], peer(2))
+
     weight_arrival.wait_recv()
     for n in range(2):
         multiply_group(0, 2 - core * 2 + n)
     shares_0 = send_shares(0, full)
-
-    from_x[0].wait_recv()
-    far_lower = remote(tokens.at[1, lower], tokens.at[3, lower], peer(4))
-    from_y[0].wait_recv()
-    far_upper = remote(tokens.at[2, upper], tokens.at[3, upper], peer(2))
 
     scale_tokens(1, 2)
     for n in range(4):

time: 100 us -> 117 us (1.17)
  Pallas kernels: 92.4 us -> 110 us
    pallas_call x1, Pallas kernels: 92.4 us -> 110 us  [on_device_fused(): pl.pallas_call(fused_kernel, out_shape=(jax.ShapeDtypeStruct((count, dept...]
where the time goes in v7:
time: 117 us; the launch traced here: 116 us
  Pallas kernels  110 us (94%)
  local copies, waits for them, and re-layouts  5.05 us (4%)
    pallas_call x1, Pallas kernels, on_device_fused(): pl.pallas_call(fused_kernel, out_shape=(jax.ShapeDtypeStruct((count, dept...  110 us
    unnamed x8, local copies, waits for them, and re-layouts  5.05 us

profile of v7, /device:TPU:12, one launch (start us, length us, event | category | flops | bytes accessed | tf_op | source)
XLA Modules:
  0.0 115.8 jit_solution(9145781696707718080)
XLA Ops:
  0.6 110.0 %shard_map.111 = (bf16[192,1024]{1,0:T(8,128)(2,1)}, f32[64,1024]{1,0:T(8,128)}, f32[64,3584]{1,0:T(8,128)}, f32[3584]{0:T(1024)}) custom-call(s32[512,3584]{1,0:T(8,128)} %codes_hbm.1, f32[56,512]{1,0:T(8,128)} %bitcast.5, bf16[64,4096]{1,0:T(8,128)(2,1)} %bitcast.3, bf16[64,3584]{1,0:T(8,128)(2,1)} %second_ref.1, f32[3584]{0:T(1024)} %magnitude_ref.1, ...), custom_call_target="tpu_custom_call" | custom-call | tf_op jit(solution)/shard_map/pallas_call | solution.py:504
  110.7 0.0 copy-start
  110.7 0.0 copy-start.1
  110.7 1.8 %copy.16 = bf16[192,1024]{1,0:T(8,128)(2,1)} copy(bf16[192,1024]{1,0:T(8,128)(2,1)} %get-tuple-element.16) | data formatting | bytes 786432
  112.6 1.7 %copy.17 = f32[1024,64]{0,1:T(8,128)} copy(f32[1024,64]{0,1:T(8,128)} %bitcast.4) | data formatting | bytes 524288
  114.2 0.0 copy-done
  114.2 0.9 copy.18
  115.2 0.0 copy-done.1
  115.2 0.6 copy.19
Async XLA Ops:
  110.7 3.5 %copy-start = (f32[64,3584]{1,0:T(8,128)S(1)}, f32[64,3584]{1,0:T(8,128)}, u32[]{:S(2)}) copy-start(f32[64,3584]{1,0:T(8,128)} %get-tuple-element.18) | copy-start | bytes 2752516
  110.7 4.5 %copy-start.1 = (f32[3584]{0:T(1024)S(1)}, f32[3584]{0:T(1024)}, u32[]{:S(2)}) copy-start(f32[3584]{0:T(1024)} %get-tuple-element.19) | copy-start | bytes 43012
